TPU v7x, 32 devices: a whole 2x2x4 slice. The times are simulated.
32 devices in a mesh: dp: 32 (over z, y, x, core), tensor: 1.
Axes of the slice: x: 2, y: 2, z: 4, core: 2. Of those that a mesh axis runs over, the one named last changes fastest.
Arguments:
- tokens: bfloat16 [4096, 14336], P('dp', 'tensor'), may hold values from -22 to 22
- frozen_matrix: bfloat16 [14336, 4096], P('tensor', 'dp')
- adapter_down_factor: bfloat16 [14336, 64], P('tensor'), may hold values from -0.046875 to 0.046875
- adapter_up_factor: bfloat16 [64, 4096], P(None, 'tensor'), may hold values from -3 to 3
- magnitude: bfloat16 [4096], P('tensor'), may hold values from 0.5 to 2
- cotangent: bfloat16 [4096, 4096], P('dp'), may hold values from -6 to 6
Outputs:
- output: bfloat16 [4096, 4096], P('dp', 'tensor')
- input_gradient: bfloat16 [4096, 14336], P('dp', 'tensor')
- grad_down: float32 [14336, 64], P('tensor')
- grad_up: float32 [64, 4096], P(None, 'tensor')
- grad_magnitude: float32 [4096], P('tensor')
All inputs are finite; a program needn't handle non-finite values.
Results may differ from a plain program's by a relative error of at most 0.0056.
Values may be sent and summed in bfloat16 or wider, within the bound.
A program may use at most 192 MiB of HBM per device.

v0:
```python
import math

import jax
import jax.numpy as jnp
from jax import lax
from jax.sharding import PartitionSpec as P

epsilon = 1e-06


def on_device(tokens, frozen_matrix, adapter_down_factor, adapter_up_factor, magnitude, cotangent):
    tok_rows = tokens.shape[0]
    local_portion = adapter_up_factor.shape[1]
    gathered_up_factor, full_magnitude = (
        lax.all_gather(adapter_up_factor, "tensor", axis=1, tiled=True),
        lax.all_gather(magnitude, "tensor", axis=0, tiled=True),
    )
    rank_partial = jnp.dot(tokens, adapter_down_factor, preferred_element_type=jnp.float32)
    rank_activation = lax.psum(rank_partial, "tensor").astype(jnp.bfloat16)
    piece = lax.all_gather(frozen_matrix, "dp", axis=1, tiled=True)
    result = jnp.dot(tokens, piece, preferred_element_type=jnp.float32)
    combined_output = piece.astype(jnp.float32) + jnp.dot(
        adapter_down_factor, gathered_up_factor, preferred_element_type=jnp.float32
    )
    squares = jnp.sum(combined_output * combined_output, axis=0)
    square_part = squares
    squares = lax.psum(square_part, "tensor")
    norm = jnp.sqrt(squares + epsilon)
    scale = full_magnitude.astype(jnp.float32) / norm
    frozen_output = lax.psum_scatter(result, "tensor", scatter_dimension=1, tiled=True)
    shard_start = lax.axis_index("tensor") * local_portion
    merged_weight = frozen_output + jnp.dot(
        rank_activation, adapter_up_factor, preferred_element_type=jnp.float32
    )
    own_scale = lax.dynamic_slice_in_dim(scale, shard_start, local_portion, 0)
    own_norm_vals = lax.dynamic_slice_in_dim(norm, shard_start, local_portion, 0)
    output = (merged_weight * own_scale).astype(jnp.bfloat16)
    rescaled_gradient = (cotangent.astype(jnp.float32) * scale).astype(jnp.bfloat16)
    rank_gradient = jnp.dot(
        rescaled_gradient, gathered_up_factor.T, preferred_element_type=jnp.float32
    ).astype(jnp.bfloat16)
    gradient_running_total = lax.dot_general(
        rescaled_gradient,
        lax.all_gather(frozen_matrix, "dp", axis=1, tiled=True),
        (((1,), (1,)), ((), ())),
        preferred_element_type=jnp.float32,
    )
    input_gradient = (
        gradient_running_total
        + jnp.dot(rank_gradient, adapter_down_factor.T, preferred_element_type=jnp.float32)
    ).astype(jnp.bfloat16)
    own_grad = lax.dynamic_slice_in_dim(rescaled_gradient, shard_start, local_portion, 1)
    own_cotangent = lax.dynamic_slice_in_dim(cotangent, shard_start, local_portion, 1).astype(
        jnp.float32
    )
    down_part = lax.dot_general(
        tokens, rank_gradient, (((0,), (0,)), ((), ())), preferred_element_type=jnp.float32
    )
    up_part = lax.dot_general(
        rank_activation, own_grad, (((0,), (0,)), ((), ())), preferred_element_type=jnp.float32
    )
    magnitude_part = jnp.sum(own_cotangent * merged_weight / own_norm_vals, axis=0)
    grad_down, grad_up, grad_magnitude = lax.psum((down_part, up_part, magnitude_part), "dp")
    factor = 1.0 / math.sqrt(tok_rows * lax.axis_size("dp"))
    return (output, input_gradient, grad_down * factor, grad_up * factor, grad_magnitude * factor)


def solution(mesh):
    return jax.shard_map(
        on_device,
        mesh=mesh,
        in_specs=(
            P("dp", "tensor"),
            P("tensor", "dp"),
            P("tensor", None),
            P(None, "tensor"),
            P("tensor"),
            P("dp", None),
        ),
        out_specs=(
            P("dp", "tensor"),
            P("dp", "tensor"),
            P("tensor", None),
            P(None, "tensor"),
            P("tensor"),
        ),
        check_vma=False,
    )
```

profile of v0, /device:TPU:0, one launch (start us, length us, event | category | flops | bytes accessed | tf_op | source)
XLA Modules:
  0.0 828.7 jit_solution(9206487931599723634)
XLA Ops:
  7.2 0.0 copy-start
  7.2 0.0 all-gather.2.cloned.1.call-start
  7.2 0.7 all-gather.2.cloned.1.call-update
  7.9 0.0 all-reduce.3.cloned.1.call-start
  8.0 0.7 copy-done
  8.7 3.4 convolution_convert_fusion.1
  12.1 0.0 copy-start.3
  12.1 0.0 copy-start.1
  12.1 612.9 %all-gather.2.cloned.1.call-done = bf16[14336,4096]{1,0:T(8,128)(2,1)} async-done(((bf16[14336,128]{1,0:T(8,128)(2,1)}), bf16[14336,4096]{1,0:T(8,128)(2,1)}) %all-gather.2.cloned.1.call-update) | async-done | bytes 117440528 | tf_op jit(solution)/shard_map/all_gather | solution.py:20
  625.1 42.0 %multiply_reduce_fusion = f32[4096]{0:T(1024)S(1)} fusion(bf16[14336,4096]{1,0:T(8,128)(2,1)} %all-gather.2.cloned.1.call-done, bf16[14336,64]{0,1:T(8,128)(2,1)S(1)} %copy-done, bf16[64,4096]{1,0:T(8,128)(2,1)S(1)} %copy-done.4), kind=kOutput, calls=%fused_computation | convolution fusion | flops 7751069696 | bytes 119816192 | tf_op jit(solution)/shard_map/dot_general | solution.py:22
  667.1 0.0 copy-done.1
  667.1 0.5 convolution_convert_fusion
  667.6 4.5 convolution_bitcast_fusion
  672.1 1.3 fusion.4
  673.4 0.0 all-reduce.3.cloned.1.call-update
  673.4 50.0 %fusion.7 = f32[128,14336]{1,0:T(8,128)} fusion(bf16[14336,4096]{1,0:T(8,128)(2,1)} %all-gather.2.cloned.1.call-done, bf16[128,4096]{1,0:T(8,128)(2,1)S(1)} %copy-done.1, f32[4096]{0:T(1024)S(1)} %get-tuple-element.10), kind=kOutput, calls=%fused_computation.15 | convolution fusion | flops 15033958400 | bytes 125845504 | tf_op jit(solution)/shard_map/dot_general | solution.py:42
  723.4 41.1 %fusion.9 = f32[128,4096]{1,0:T(8,128)} fusion(bf16[128,14336]{1,0:T(8,128)(2,1)} %param.6, bf16[14336,4096]{1,0:T(8,128)(2,1)} %all-gather.2.cloned.1.call-done), kind=kOutput, calls=%fused_computation.20 | convolution fusion | flops 15032385536 | bytes 123207680 | tf_op jit(solution)/shard_map/dot_general | solution.py:21
  764.5 3.3 fusion.3
  767.8 38.5 %psum.24 = f32[4096]{0:T(1024)S(1)} all-reduce(f32[4096]{0:T(1024)S(1)} %get-tuple-element.7), channel_id=1, replica_groups=mesh['dp'=32,'tensor'=1] {'dp'}, use_global_device_ids=true, to_apply=%region_4.0 | all-reduce | flops 4096 | bytes 32768 | tf_op jit(solution)/shard_map/psum | solution.py:63
  806.3 0.6 broadcast_multiply_fusion.2
  806.9 6.1 fusion
  813.0 3.5 all-reduce.3.cloned.1.call-done
  816.5 4.2 broadcast_multiply_fusion
  820.8 1.1 broadcast_multiply_fusion.1
  (6 shorter events, 0.0 us)
Async XLA Ops:
  7.2 1.5 copy-start
  7.2 617.9 %all-gather.2.cloned.1.call-start = ((), (), s32[]{:S(2)}) async-start(), calls=%async_computation | async-start | bytes 121110528 | tf_op jit(solution)/shard_map/all_gather | solution.py:20
  7.9 617.2 %copy-start.4 = (bf16[64,4096]{1,0:T(8,128)(2,1)S(1)}, bf16[64,4096]{1,0:T(8,128)(2,1)}, u32[]{:S(2)}) copy-start(bf16[64,4096]{1,0:T(8,128)(2,1)} %param.9) | copy-start | bytes 1572868
  7.9 808.6 %all-reduce.3.cloned.1.call-start = ((), (), s32[]{:S(2)}) async-start(), calls=%async_computation.1 | async-start | bytes 9437184 | tf_op jit(solution)/shard_map/psum | solution.py:63
  12.1 654.9 %copy-start.3 = (bf16[4096]{0:T(1024)(128)(2,1)S(1)}, bf16[4096]{0:T(1024)(128)(2,1)}, u32[]{:S(2)}) copy-start(bf16[4096]{0:T(1024)(128)(2,1)} %param.10) | copy-start | bytes 24580
  12.1 655.0 %copy-start.1 = (bf16[128,4096]{1,0:T(8,128)(2,1)S(1)}, bf16[128,4096]{1,0:T(8,128)(2,1)}, u32[]{:S(2)}) copy-start(bf16[128,4096]{1,0:T(8,128)(2,1)} %param.11) | copy-start | bytes 3145732
  816.5 4.2 copy-start.2
Sparse Core Ops, SparseCore 0:
  9.5 615.4 all-gather.1
  673.5 142.9 all-reduce.2
where the time goes:
time: 829 us
  waiting for transfers between devices  617 us (74%)
  matrix products  152 us (18%)
  blocking collectives  38.5 us (5%)
  between operations  14.1 us (2%)
    all_gather x1, waiting for transfers between devices, on_device(): piece = lax.all_gather(frozen_matrix, 'dp', axis=1, tiled=True)  613 us
    dot_general x1, matrix products, on_device(): lax.dot_general(rescaled_gradient, lax.all_gather(frozen_matrix, 'dp', ax...  50 us
    dot_general x1, matrix products, on_device(): jnp.dot(adapter_down_factor, gathered_up_factor, preferred_element_type=j...  42 us
    dot_general x1, matrix products, on_device(): result = jnp.dot(tokens, piece, preferred_element_type=jnp.float32)  41.1 us
    psum x1, blocking collectives, on_device(): lax.psum((down_part, up_part, magnitude_part), 'dp')  38.5 us
  transfers between devices with their start and end apart: 2, of which 2 were waited for; matrix products, arithmetic and copies ran while one was open for 13% of the time, Pallas kernels for 0%

commit v1 on v0

--- a/solution.py
+++ b/solution.py
@@ -1,11 +1,230 @@
+import functools
 import math
 
 import jax
 import jax.numpy as jnp
 from jax import lax
+from jax.experimental import pallas as pl
+from jax.experimental.pallas import tpu as pltpu
 from jax.sharding import PartitionSpec as P
 
 epsilon = 1e-06
+
+CHIPS = 4
+CORES = 2
+PLANE = CHIPS * CORES
+
+
+def place():
+    me = lax.axis_index("dp")
+    return me // PLANE, (me % PLANE) // CORES, me % CORES
+
+
+def exchange_kernel(views, count, *refs):
+    sources, targets = refs[:count], refs[count : 2 * count]
+    send_sem, recv_sem, local_sem = refs[2 * count :]
+    me = lax.axis_index("dp")
+    chip = (me % PLANE) // CORES
+    base = me - chip * CORES
+    barrier = pltpu.get_barrier_semaphore()
+    for hop in range(1, CHIPS):
+        pl.semaphore_signal(
+            barrier, inc=1, device_id={"dp": base + ((chip + hop) % CHIPS) * CORES},
+            device_id_type=pl.DeviceIdType.MESH,
+        )
+    pl.semaphore_wait(barrier, CHIPS - 1)
+    copies = []
+    for number, view in enumerate(views):
+        for hop in (2, 1, 3):
+            other = (chip + hop) % CHIPS
+            source, target = view(sources[number], targets[number], other, chip)
+            copies.append(
+                pltpu.make_async_remote_copy(
+                    src_ref=source, dst_ref=target,
+                    send_sem=send_sem.at[number, hop], recv_sem=recv_sem.at[number, hop],
+                    device_id={"dp": base + other * CORES},
+                    device_id_type=pl.DeviceIdType.MESH,
+                )
+            )
+            copies[-1].start()
+    for number, view in enumerate(views):
+        source, target = view(sources[number], targets[number], chip, chip)
+        copies.append(pltpu.make_async_copy(source, target, local_sem.at[number]))
+        copies[-1].start()
+    for copy in copies:
+        copy.wait()
+
+
+def exchange(views, sources, shapes, collective_id):
+    count = len(views)
+    moved = sum(math.prod(s.shape) * s.dtype.itemsize for s in shapes)
+    return pl.pallas_call(
+        functools.partial(exchange_kernel, views, count),
+        out_shape=list(shapes),
+        in_specs=[pl.BlockSpec(memory_space=pl.ANY)] * count,
+        out_specs=[pl.BlockSpec(memory_space=pl.ANY)] * count,
+        scratch_shapes=[
+            pltpu.SemaphoreType.DMA((count, CHIPS)),
+            pltpu.SemaphoreType.DMA((count, CHIPS)),
+            pltpu.SemaphoreType.DMA((count,)),
+        ],
+        compiler_params=pltpu.CompilerParams(
+            collective_id=collective_id, has_side_effects=True
+        ),
+        cost_estimate=pl.CostEstimate(flops=0, bytes_accessed=40 * moved, transcendentals=0),
+    )(*sources)
+
+
+def rows_to_columns(depth):
+    def view(source, target, other, chip):
+        rows = source.shape[0]
+        return (
+            source.at[:, pl.ds(pl.multiple_of(other * depth, 128), depth)],
+            target.at[pl.ds(pl.multiple_of(chip * rows, 128), rows), :],
+        )
+    return view
+
+
+def columns_to_rows(rows, depth):
+    def view(source, target, other, chip):
+        return (
+            source.at[pl.ds(pl.multiple_of(other * rows, 128), rows), :],
+            target.at[:, pl.ds(pl.multiple_of(chip * depth, 128), depth)],
+        )
+    return view
+
+
+def whole_rows(source, target, other, chip):
+    rows = source.shape[0]
+    return source, target.at[pl.ds(pl.multiple_of(chip * rows, 128), rows), :]
+
+
+def rows_to_slots(rows):
+    def view(source, target, other, chip):
+        return source.at[pl.ds(pl.multiple_of(other * rows, 128), rows), :], target.at[chip]
+    return view
+
+
+def frozen_view(depth, width):
+    def view(source, target, other, chip):
+        return (
+            source.at[pl.ds(pl.multiple_of(other * depth, 128), depth), :],
+            target.at[chip // 2, :, pl.ds(pl.multiple_of((chip % 2) * width, 128), width)],
+        )
+    return view
+
+
+def dot(a, b, contract):
+    return lax.dot_general(a, b, ((contract[:1], contract[1:]), ((), ())),
+                           preferred_element_type=jnp.float32)
+
+
+def on_plane(tokens, frozen, down, up, magnitude, cotangent):
+    rows, features = tokens.shape
+    width = frozen.shape[1]
+    outputs = cotangent.shape[1]
+    size = lax.axis_size("dp")
+    planes = size // PLANE
+    depth = features // CHIPS
+    half = outputs // planes // 2
+    me = lax.axis_index("dp")
+    plane, chip, core = place()
+    f32, bf16 = jnp.float32, jnp.bfloat16
+
+    (blocks,) = exchange(
+        [frozen_view(depth, width)], [frozen],
+        [jax.ShapeDtypeStruct((2, depth, 2 * width), bf16)], 1,
+    )
+    blocks, tokens, frozen, cotangent = lax.optimization_barrier(
+        (blocks, tokens, frozen, cotangent)
+    )
+
+    forward = [(i, (i + PLANE) % size) for i in range(size)]
+    backward = [((i + PLANE) % size, i) for i in range(size)]
+    across = [(i, i - i % CORES + (i + 1) % CORES) for i in range(size)]
+    pieces = [[blocks[0], blocks[1]]]
+    for step in range(planes - 1):
+        pieces.append([
+            lax.ppermute(pieces[-1][0], "dp", forward),
+            lax.ppermute(pieces[-1][1], "dp", backward),
+        ])
+    others = [[lax.ppermute(part, "dp", across) for part in pair] for pair in pieces]
+
+    tokens_part, cotangent_part = exchange(
+        [rows_to_columns(depth), whole_rows], [tokens, cotangent],
+        [jax.ShapeDtypeStruct((CHIPS * rows, depth), bf16),
+         jax.ShapeDtypeStruct((CHIPS * rows, outputs), bf16)], 2,
+    )
+
+    own_up = lax.dynamic_slice_in_dim(up, me * width, width, 1)
+    combined = frozen.astype(f32) + jnp.dot(down, own_up, preferred_element_type=f32)
+    squares = lax.all_gather(jnp.sum(combined * combined, axis=0), "dp", axis=0, tiled=True)
+    norm = jnp.sqrt(squares + epsilon)
+    scale = magnitude.astype(f32) / norm
+
+    rank_act = jnp.dot(tokens, down, preferred_element_type=f32).astype(bf16)
+    adapter = jnp.dot(rank_act, up, preferred_element_type=f32)
+    cot_own = cotangent.astype(f32)
+    grad_own = (cot_own * scale).astype(bf16)
+    back_own = dot(grad_own, up, (1, 1)).astype(bf16)
+    factor = 1.0 / math.sqrt(rows * size)
+    down_part = dot(tokens, back_own, (0, 0))
+    up_part = dot(rank_act, grad_own, (0, 0))
+    grad_down, grad_up = lax.psum((down_part, up_part), "dp")
+
+    grad_part = (cotangent_part.astype(f32) * scale).astype(bf16)
+    back_part = dot(grad_part, up, (1, 1)).astype(bf16)
+    down_rows = lax.dynamic_slice_in_dim(down, chip * depth, depth, 0)
+    gradient = dot(back_part, down_rows, (1, 1))
+
+    partial, sums = [], []
+    for step in range(planes):
+        for side in range(2):
+            where = (plane + (planes - step if side == 0 else step)) % planes
+            start = where * 2 * half + side * half
+            group = (CHIPS * rows, 2, CORES, width)
+            cot = lax.dynamic_slice_in_dim(cotangent_part, start, half, 1)
+            grad = lax.dynamic_slice_in_dim(grad_part, start, half, 1).reshape(group)
+            outs = []
+            for part, kind in ((pieces[step][side], core), (others[step][side], 1 - core)):
+                outs.append(dot(tokens_part, part, (1, 0)))
+                grad_kind = lax.dynamic_index_in_dim(grad, kind, 2, False)
+                grad_kind = grad_kind.reshape(CHIPS * rows, 2 * width)
+                gradient = gradient + dot(grad_kind, part, (1, 1))
+            first = jnp.where(core == 0, outs[0], outs[1]).reshape(CHIPS * rows, 2, 1, width)
+            second = jnp.where(core == 0, outs[1], outs[0]).reshape(CHIPS * rows, 2, 1, width)
+            out = jnp.concatenate([first, second], axis=2).reshape(CHIPS * rows, half)
+            sums.append(jnp.sum(cot.astype(f32) * out, axis=0))
+            partial.append(out.astype(bf16))
+
+    early = jnp.concatenate(partial[:-2], axis=1)
+    late = jnp.concatenate(partial[-2:], axis=1)
+    (early_slots,) = exchange(
+        [rows_to_slots(rows)], [early],
+        [jax.ShapeDtypeStruct((CHIPS, rows, early.shape[1]), bf16)], 3,
+    )
+    late_slots, input_gradient = exchange(
+        [rows_to_slots(rows), columns_to_rows(rows, depth)], [late, gradient.astype(bf16)],
+        [jax.ShapeDtypeStruct((CHIPS, rows, late.shape[1]), bf16),
+         jax.ShapeDtypeStruct((rows, features), bf16)], 4,
+    )
+
+    def in_order(steps):
+        lead = steps.shape[:-1]
+        steps = steps.reshape(lead + (planes, 2, half))
+        number = jnp.arange(planes)
+        falling = jnp.take(steps[..., 0, :], (plane - number) % planes, axis=-2)
+        rising = jnp.take(steps[..., 1, :], (number - plane) % planes, axis=-2)
+        return jnp.stack([falling, rising], axis=-2).reshape(lead + (outputs,))
+
+    sums = in_order(jnp.concatenate(sums)) + jnp.sum(cot_own * adapter, axis=0)
+    grad_magnitude = jnp.sum(lax.all_gather(sums / norm, "dp"), axis=0)
+
+    base = jnp.concatenate(
+        [jnp.sum(early_slots.astype(f32), axis=0), jnp.sum(late_slots.astype(f32), axis=0)], axis=1
+    )
+    output = ((in_order(base) + adapter) * scale).astype(bf16)
+    return (output, input_gradient, grad_down * factor, grad_up * factor, grad_magnitude * factor)
 
 
 def on_device(tokens, frozen_matrix, adapter_down_factor, adapter_up_factor, magnitude, cotangent):
@@ -66,8 +285,10 @@
 
 
 def solution(mesh):
+    planes = mesh.shape["dp"] // PLANE
+    in_planes = mesh.shape["tensor"] == 1 and mesh.shape["dp"] == PLANE * planes and planes > 1
     return jax.shard_map(
-        on_device,
+        on_plane if in_planes else on_device,
         mesh=mesh,
         in_specs=(
             P("dp", "tensor"),

time: 829 us -> 798 us (0.963)
  waiting for transfers between devices: 617 us -> 39 us
  Pallas kernels: 0 us -> 238 us
  blocking collectives: 38.5 us -> 142 us
  local copies, waits for them, and re-layouts: 0.73 us -> 89.9 us
  matrix products: 152 us -> 207 us
  other arithmetic: 5.9 us -> 49.3 us
  starting transfers between devices: 0.08 us -> 13.6 us
    all_gather x1 -> x0, waiting for transfers between devices: 613 us -> none  [on_device(): piece = lax.all_gather(frozen_matrix, 'dp', axis=1, tiled=True)]
    pallas_call x0 -> x4, Pallas kernels: none -> 238 us  [exchange(): pl.pallas_call(functools.partial(exchange_kernel, views, count), out_shap...]
    all_gather x0 -> x2, blocking collectives: none -> 142 us  [the longest x1 102 us: on_plane(): lax.all_gather(jnp.sum(combined * combined, axis=0), 'dp', axis=0, tiled=...]
    dot_general x9 -> x38, matrix products: 152 us -> 207 us  [the longest x35 199 us: dot(): lax.dot_general(a, b, ((contract[:1], contract[1:]), ((), ())), preferred...]
    psum x1 -> x0, blocking collectives: 38.5 us -> none  [on_device(): lax.psum((down_part, up_part, magnitude_part), 'dp')]
    reshape x0 -> x26, local copies, waits for them, and re-layouts: none -> 37.6 us  [the longest x8 21.2 us: on_plane(): out = jnp.concatenate([first, second], axis=2).reshape(CHIPS * rows, half)]
    dynamic_slice x0 -> x13, local copies, waits for them, and re-layouts: none -> 24.3 us  [the longest x9 17.8 us: on_plane(): grad = lax.dynamic_slice_in_dim(grad_part, start, half, 1).reshape(group)]
    ppermute x0 -> x14, waiting for transfers between devices: none -> 22.8 us  [the longest x3 22.8 us: on_plane(): lax.ppermute(pieces[-1][1], 'dp', backward)]
  transfers between devices with their start and end apart: 2 -> 15, of which waited for: 2 -> 3; matrix products, arithmetic and copies ran while one was open for 13% -> 31% of each run, Pallas kernels for 0% -> 18%
where the time goes in v1:
time: 798 us; the launch traced here: 794 us
  Pallas kernels  238 us (30%)
  matrix products  207 us (26%)
  blocking collectives  142 us (18%)
  local copies, waits for them, and re-layouts  89.9 us (11%)
  other arithmetic  49.3 us (6%)
  waiting for transfers between devices  39 us (5%)
  between operations  15.2 us (2%)
  starting transfers between devices  13.6 us (2%)
    pallas_call x4, Pallas kernels, exchange(): pl.pallas_call(functools.partial(exchange_kernel, views, count), out_shap...  238 us
    dot_general x35, matrix products, dot(): lax.dot_general(a, b, ((contract[:1], contract[1:]), ((), ())), preferred...  199 us
    all_gather x1, blocking collectives, on_plane(): lax.all_gather(jnp.sum(combined * combined, axis=0), 'dp', axis=0, tiled=...  102 us
    all_gather x1, blocking collectives, on_plane(): grad_magnitude = jnp.sum(lax.all_gather(sums / norm, 'dp'), axis=0)  39.8 us
    ppermute x3, waiting for transfers between devices, on_plane(): lax.ppermute(pieces[-1][1], 'dp', backward)  22.8 us
    reshape x8, local copies, waits for them, and re-layouts, on_plane(): out = jnp.concatenate([first, second], axis=2).reshape(CHIPS * rows, half)  21.2 us
    dynamic_slice x9, local copies, waits for them, and re-layouts, on_plane(): grad = lax.dynamic_slice_in_dim(grad_part, start, half, 1).reshape(group)  17.8 us
    psum x1, waiting for transfers between devices, on_plane(): grad_down, grad_up = lax.psum((down_part, up_part), 'dp')  16.2 us
  transfers between devices with their start and end apart: 15, of which 3 were waited for; matrix products, arithmetic and copies ran while one was open for 31% of the time, Pallas kernels for 18%

profile of v1, /device:TPU:0, one launch (start us, length us, event | category | flops | bytes accessed | tf_op | source)
XLA Modules:
  0.0 793.9 jit_solution(15598567845529897567)
XLA Ops:
  7.2 44.7 %shard_map.101 = bf16[2,3584,256]{2,1,0:T(8,128)(2,1)} custom-call(bf16[14336,128]{1,0:T(8,128)(2,1)} %refs_0_.1), custom_call_target="tpu_custom_call" | custom-call | bytes 146800640 | tf_op jit(solution)/shard_map/pallas_call | solution.py:61
  60.1 6.1 copy.128
  69.8 101.8 %all-gather.1 = f32[32,1,128]{2,1,0:T(1,128)S(1)} all-gather(f32[1,1,128]{2,1,0:T(1,128)S(1)} %bitcast.198), channel_id=1, replica_groups=mesh['dp'=32,'tensor'=1] {'dp'}, dimensions={0}, use_global_device_ids=true | all-gather | bytes 16896 | tf_op jit(solution)/shard_map/all_gather | solution.py:161
  179.9 102.0 %shard_map.102 = (bf16[512,3584]{1,0:T(8,128)(2,1)}, bf16[512,4096]{1,0:T(8,128)(2,1)}) custom-call(bf16[128,14336]{1,0:T(8,128)(2,1)} %refs_0_.2, bf16[128,4096]{1,0:T(8,128)(2,1)} %refs_1_), custom_call_target="tpu_custom_call" | custom-call | bytes 314572800 | tf_op jit(solution)/shard_map/pallas_call | solution.py:61
  317.3 5.8 fusion.19
  324.3 7.7 fusion.5
  364.9 5.7 fusion.29
  370.6 5.7 fusion.30
  376.3 5.7 fusion.31
  387.6 16.2 %all-reduce.3.cloned.1.call-done = (f32[14336,64]{0,1:T(8,128)}, f32[64,4096]{1,0:T(8,128)}) async-done(((f32[14336,64]{0,1:T(8,128)}, f32[64,4096]{1,0:T(8,128)}), (f32[14336,64]{0,1:T(8,128)}, f32[64,4096]{1,0:T(8,128)})) %all-reduce.3.cloned.1.call-update) | async-done | bytes 4718608 | tf_op jit(solution)/shard_map/psum | solution.py:173
  422.0 17.9 %collective-permute-done.8 = bf16[3584,256]{1,0:T(8,128)(2,1)} collective-permute-done((bf16[3584,256]{1,0:T(8,128)(2,1)}, bf16[3584,256]{1,0:T(8,128)(2,1)}, u32[]{:S(2)}, u32[]{:S(2)}) %collective-permute-start.8) | collective-permute-done | bytes 1835040 | tf_op jit(solution)/shard_map/ppermute | solution.py:149
  442.1 5.7 fusion.32
  453.4 5.7 fusion.37
  459.2 5.9 fusion.34
  520.1 5.6 fusion.36
  525.8 5.7 fusion.38
  535.9 37.2 %shard_map.103 = bf16[4,128,3072]{2,1,0:T(8,128)(2,1)} custom-call(bf16[512,3072]{1,0:T(8,128)(2,1)} %convert_dynamic-update-slice_fusion.refs_0_), custom_call_target="tpu_custom_call" | custom-call | bytes 125829120 | tf_op jit(solution)/shard_map/pallas_call | solution.py:61
  577.0 5.7 fusion.39
  582.6 5.9 fusion.41
  610.0 6.3 multiply_reduce_fusion
  618.9 5.6 fusion.40
  624.5 37.9 %add_convert_fusion.refs_1_ = bf16[512,3584]{1,0:T(8,128)(2,1)} fusion(f32[512,3584]{1,0:T(8,128)} %fusion.41, f32[512,3584]{1,0:T(8,128)} %fusion.40, f32[512,3584]{1,0:T(8,128)} %fusion.39, f32[512,3584]{1,0:T(8,128)} %fusion.38, f32[512,3584]{1,0:T(8,128)} %fusion.37, f32[512,3584]{1,0:T(8,128)} %fusion.36, f32[512,3584]{1,0:T(8,128)} %fusion.35, ...), kind=kOutput, calls=%fused_computation.8 | convolution fusion | flops 970719232 | bytes 123207680 | tf_op jit(solution)/shard_map/dot_general | solution.py:118
  662.5 54.3 %shard_map.104 = (bf16[4,128,1024]{2,1,0:T(8,128)(2,1)}, bf16[128,14336]{1,0:T(8,128)(2,1)}) custom-call(bf16[512,1024]{1,0:T(8,128)(2,1)} %pad_maximum_fusion.10.refs_0_, bf16[512,3584]{1,0:T(8,128)(2,1)} %add_convert_fusion.refs_1_), custom_call_target="tpu_custom_call" | custom-call | bytes 188743680 | tf_op jit(solution)/shard_map/pallas_call | solution.py:61
  741.9 39.8 %all-gather = f32[131072]{0:T(1024)S(1)} all-gather(f32[4096]{0:T(1024)S(1)} %add_divide_fusion), channel_id=2, replica_groups=mesh['dp'=32,'tensor'=1] {'dp'}, dimensions={0}, use_global_device_ids=true | all-gather | bytes 540672 | tf_op jit(solution)/shard_map/all_gather | solution.py:221
  (251 shorter events, 238.2 us)
Async XLA Ops:
  7.2 59.1 %copy-start = (bf16[14336,64]{0,1:T(8,128)(2,1)S(1)}, bf16[14336,64]{0,1:T(8,128)(2,1)}, u32[]{:S(2)}) copy-start(bf16[14336,64]{0,1:T(8,128)(2,1)} %param.12) | copy-start | bytes 5505028
  7.2 396.6 %all-reduce.3.cloned.1.call-start = ((), (), s32[]{:S(2)}) async-start(), calls=%async_computation | async-start | bytes 9437184 | tf_op jit(solution)/shard_map/psum | solution.py:173
  56.0 280.7 %collective-permute-start = (bf16[3584,256]{1,0:T(8,128)(2,1)}, bf16[3584,256]{1,0:T(8,128)(2,1)}, u32[]{:S(2)}, u32[]{:S(2)}) collective-permute-start(bf16[3584,256]{1,0:T(8,128)(2,1)} %get-tuple-element.41), channel_id=1, source_target_pairs={{0,1},{1,0},{2,3},{3,2},{4,5},{5,4},{6,7},{7,6},{8,9},{9,8},{10,11... | collective-permute-start | bytes 5505032 | tf_op jit(solution)/shard_map/ppermute | solution.py:151
  56.0 295.5 %collective-permute-start.2 = (bf16[3584,256]{1,0:T(8,128)(2,1)}, bf16[3584,256]{1,0:T(8,128)(2,1)}, u32[]{:S(2)}, u32[]{:S(2)}) collective-permute-start(bf16[3584,256]{1,0:T(8,128)(2,1)} %get-tuple-element.41), channel_id=1, source_target_pairs={{0,8},{1,9},{2,10},{3,11},{4,12},{5,13},{6,14},{7,15},{8,16},{9,17... | collective-permute-start | bytes 5505032 | tf_op jit(solution)/shard_map/ppermute | solution.py:148
  57.6 284.4 %collective-permute-start.1 = (bf16[3584,256]{1,0:T(8,128)(2,1)}, bf16[3584,256]{1,0:T(8,128)(2,1)}, u32[]{:S(2)}, u32[]{:S(2)}) collective-permute-start(bf16[3584,256]{1,0:T(8,128)(2,1)} %get-tuple-element.42), channel_id=1, source_target_pairs={{0,1},{1,0},{2,3},{3,2},{4,5},{5,4},{6,7},{7,6},{8,9},{9,8},{10,11... | collective-permute-start | bytes 5505032 | tf_op jit(solution)/shard_map/ppermute | solution.py:151
  57.8 299.3 %collective-permute-start.4 = (bf16[3584,256]{1,0:T(8,128)(2,1)}, bf16[3584,256]{1,0:T(8,128)(2,1)}, u32[]{:S(2)}, u32[]{:S(2)}) collective-permute-start(bf16[3584,256]{1,0:T(8,128)(2,1)} %get-tuple-element.42), channel_id=1, source_target_pairs={{8,0},{9,1},{10,2},{11,3},{12,4},{13,5},{14,6},{15,7},{16,8},{17,9... | collective-permute-start | bytes 5505032 | tf_op jit(solution)/shard_map/ppermute | solution.py:149
  66.3 105.4 %copy-start.3 = (bf16[128,14336]{1,0:T(8,128)(2,1)S(1)}, bf16[128,14336]{1,0:T(8,128)(2,1)}, u32[]{:S(2)}) copy-start(bf16[128,14336]{1,0:T(8,128)(2,1)} %refs_0_.2) | copy-start | bytes 11010052
  69.8 103.3 %copy-start.36 = (bf16[4096]{0:T(1024)(128)(2,1)S(1)}, bf16[4096]{0:T(1024)(128)(2,1)}, u32[]{:S(2)}) copy-start(bf16[4096]{0:T(1024)(128)(2,1)} %param.14) | copy-start | bytes 24580
  69.8 103.3 %copy-start.4 = (bf16[128,4096]{1,0:T(8,128)(2,1)S(1)}, bf16[128,4096]{1,0:T(8,128)(2,1)}, u32[]{:S(2)}) copy-start(bf16[128,4096]{1,0:T(8,128)(2,1)} %refs_1_) | copy-start | bytes 3145732
  173.1 109.0 %copy-start.30 = (f32[4096]{0:T(1024)}, f32[4096]{0:T(1024)S(1)}, u32[]{:S(2)}) copy-start(f32[4096]{0:T(1024)S(1)} %convert_divide_fusion) | copy-start | bytes 49156
  351.5 9.9 %copy-start.39 = (bf16[512,3584]{1,0:T(8,128)(2,1)S(1)}, bf16[512,3584]{1,0:T(8,128)(2,1)}, u32[]{:S(2)}) copy-start(bf16[512,3584]{1,0:T(8,128)(2,1)} %get-tuple-element.17) | copy-start | bytes 11010052
  357.2 52.0 %collective-permute-start.3 = (bf16[3584,256]{1,0:T(8,128)(2,1)}, bf16[3584,256]{1,0:T(8,128)(2,1)}, u32[]{:S(2)}, u32[]{:S(2)}) collective-permute-start(bf16[3584,256]{1,0:T(8,128)(2,1)} %collective-permute-done.2), channel_id=1, source_target_pairs={{0,1},{1,0},{2,3},{3,2},{4,5},{5,4},{6,7},{7,6},{8,9},{9,8},{10,11... | collective-permute-start | bytes 5505032 | tf_op jit(solution)/shard_map/ppermute | solution.py:151
  357.2 62.1 %collective-permute-start.6 = (bf16[3584,256]{1,0:T(8,128)(2,1)}, bf16[3584,256]{1,0:T(8,128)(2,1)}, u32[]{:S(2)}, u32[]{:S(2)}) collective-permute-start(bf16[3584,256]{1,0:T(8,128)(2,1)} %collective-permute-done.2), channel_id=1, source_target_pairs={{0,8},{1,9},{2,10},{3,11},{4,12},{5,13},{6,14},{7,15},{8,16},{9,17... | collective-permute-start | bytes 5505032 | tf_op jit(solution)/shard_map/ppermute | solution.py:148
  357.2 102.0 %collective-permute-start.5 = (bf16[3584,256]{1,0:T(8,128)(2,1)}, bf16[3584,256]{1,0:T(8,128)(2,1)}, u32[]{:S(2)}, u32[]{:S(2)}) collective-permute-start(bf16[3584,256]{1,0:T(8,128)(2,1)} %collective-permute-done.4), channel_id=1, source_target_pairs={{0,1},{1,0},{2,3},{3,2},{4,5},{5,4},{6,7},{7,6},{8,9},{9,8},{10,11... | collective-permute-start | bytes 5505032 | tf_op jit(solution)/shard_map/ppermute | solution.py:151
  357.7 82.2 %collective-permute-start.8 = (bf16[3584,256]{1,0:T(8,128)(2,1)}, bf16[3584,256]{1,0:T(8,128)(2,1)}, u32[]{:S(2)}, u32[]{:S(2)}) collective-permute-start(bf16[3584,256]{1,0:T(8,128)(2,1)} %collective-permute-done.4), channel_id=1, source_target_pairs={{8,0},{9,1},{10,2},{11,3},{12,4},{13,5},{14,6},{15,7},{16,8},{17,9... | collective-permute-start | bytes 5505032 | tf_op jit(solution)/shard_map/ppermute | solution.py:149
  412.6 29.5 %copy-start.22 = (bf16[512,2,1,128]{0,3,2,1:T(8,128)(2,1)S(1)}, bf16[512,2,1,128]{0,3,2,1:T(8,128)(2,1)}, u32[]{:S(2)}) copy-start(bf16[512,2,1,128]{0,3,2,1:T(8,128)(2,1)} %get-tuple-element.91) | copy-start | bytes 786436
  419.3 67.5 %collective-permute-start.7 = (bf16[3584,256]{1,0:T(8,128)(2,1)}, bf16[3584,256]{1,0:T(8,128)(2,1)}, u32[]{:S(2)}, u32[]{:S(2)}) collective-permute-start(bf16[3584,256]{1,0:T(8,128)(2,1)} %collective-permute-done.6), channel_id=1, source_target_pairs={{0,1},{1,0},{2,3},{3,2},{4,5},{5,4},{6,7},{7,6},{8,9},{9,8},{10,11... | collective-permute-start | bytes 5505032 | tf_op jit(solution)/shard_map/ppermute | solution.py:151
  419.3 89.0 %collective-permute-start.10 = (bf16[3584,256]{1,0:T(8,128)(2,1)}, bf16[3584,256]{1,0:T(8,128)(2,1)}, u32[]{:S(2)}, u32[]{:S(2)}) collective-permute-start(bf16[3584,256]{1,0:T(8,128)(2,1)} %collective-permute-done.6), channel_id=1, source_target_pairs={{0,8},{1,9},{2,10},{3,11},{4,12},{5,13},{6,14},{7,15},{8,16},{9,17... | collective-permute-start | bytes 5505032 | tf_op jit(solution)/shard_map/ppermute | solution.py:148
  439.9 56.9 %collective-permute-start.9 = (bf16[3584,256]{1,0:T(8,128)(2,1)}, bf16[3584,256]{1,0:T(8,128)(2,1)}, u32[]{:S(2)}, u32[]{:S(2)}) collective-permute-start(bf16[3584,256]{1,0:T(8,128)(2,1)} %collective-permute-done.8), channel_id=1, source_target_pairs={{0,1},{1,0},{2,3},{3,2},{4,5},{5,4},{6,7},{7,6},{8,9},{9,8},{10,11... | collective-permute-start | bytes 5505032 | tf_op jit(solution)/shard_map/ppermute | solution.py:151
  439.9 80.2 %collective-permute-start.12 = (bf16[3584,256]{1,0:T(8,128)(2,1)}, bf16[3584,256]{1,0:T(8,128)(2,1)}, u32[]{:S(2)}, u32[]{:S(2)}) collective-permute-start(bf16[3584,256]{1,0:T(8,128)(2,1)} %collective-permute-done.8), channel_id=1, source_target_pairs={{8,0},{9,1},{10,2},{11,3},{12,4},{13,5},{14,6},{15,7},{16,8},{17,9... | collective-permute-start | bytes 5505032 | tf_op jit(solution)/shard_map/ppermute | solution.py:149
  508.3 80.2 %collective-permute-start.11 = (bf16[3584,256]{1,0:T(8,128)(2,1)}, bf16[3584,256]{1,0:T(8,128)(2,1)}, u32[]{:S(2)}, u32[]{:S(2)}) collective-permute-start(bf16[3584,256]{1,0:T(8,128)(2,1)} %collective-permute-done.10), channel_id=1, source_target_pairs={{0,1},{1,0},{2,3},{3,2},{4,5},{5,4},{6,7},{7,6},{8,9},{9,8},{10,11... | collective-permute-start | bytes 5505032 | tf_op jit(solution)/shard_map/ppermute | solution.py:151
  510.6 9.5 %copy-start.20 = (bf16[512,2,1,128]{0,3,2,1:T(8,128)(2,1)S(1)}, bf16[512,2,1,128]{0,3,2,1:T(8,128)(2,1)}, u32[]{:S(2)}) copy-start(bf16[512,2,1,128]{0,3,2,1:T(8,128)(2,1)} %get-tuple-element.89) | copy-start | bytes 786436
  520.1 78.7 %collective-permute-start.13 = (bf16[3584,256]{1,0:T(8,128)(2,1)}, bf16[3584,256]{1,0:T(8,128)(2,1)}, u32[]{:S(2)}, u32[]{:S(2)}) collective-permute-start(bf16[3584,256]{1,0:T(8,128)(2,1)} %collective-permute-done.12), channel_id=1, source_target_pairs={{0,1},{1,0},{2,3},{3,2},{4,5},{5,4},{6,7},{7,6},{8,9},{9,8},{10,11... | collective-permute-start | bytes 5505032 | tf_op jit(solution)/shard_map/ppermute | solution.py:151
  662.5 55.8 %copy-start.9 = (f32[128,3072]{1,0:T(8,128)S(1)}, f32[128,3072]{1,0:T(8,128)}, u32[]{:S(2)}) copy-start(f32[128,3072]{1,0:T(8,128)} %convert_reduce_fusion) | copy-start | bytes 4718596
  (40 other events, 202.5 us)
Sparse Core Ops, SparseCore 0:
  180.0 223.7 all-reduce.2

commit v2 on v1

--- a/solution.py
+++ b/solution.py
@@ -20,59 +20,163 @@
     return me // PLANE, (me % PLANE) // CORES, me % CORES
 
 
-def exchange_kernel(views, count, *refs):
-    sources, targets = refs[:count], refs[count : 2 * count]
-    send_sem, recv_sem, local_sem = refs[2 * count :]
+def exchange_kernel(views, vector, *refs):
+    count = len(views)
+    ends = count + (vector is not None)
+    sources, targets = refs[:count], refs[ends : ends + count]
+    small_in, small_out = refs[ends - 1], refs[2 * ends - 1]
+    scratch = refs[2 * ends :]
+    send_sem, recv_sem, local_sem = scratch[:3]
     me = lax.axis_index("dp")
-    chip = (me % PLANE) // CORES
+    planes = lax.axis_size("dp") // PLANE
+    plane, chip, core = place()
+    spot = me % PLANE
     base = me - chip * CORES
+
+    def remote(source, target, send, recv, device):
+        return pltpu.make_async_remote_copy(
+            src_ref=source, dst_ref=target, send_sem=send, recv_sem=recv,
+            device_id={"dp": device}, device_id_type=pl.DeviceIdType.MESH,
+        )
+
+    if vector is None:
+        partners = [base + ((chip + hop) % CHIPS) * CORES for hop in range(1, CHIPS)]
+    else:
+        above = [(plane + hop) % planes * PLANE + spot for hop in range(1, planes)]
+        beside = [plane * PLANE + (spot + hop) % PLANE for hop in range(1, PLANE)]
+        partners = above + beside
     barrier = pltpu.get_barrier_semaphore()
-    for hop in range(1, CHIPS):
+    for device in partners:
         pl.semaphore_signal(
-            barrier, inc=1, device_id={"dp": base + ((chip + hop) % CHIPS) * CORES},
-            device_id_type=pl.DeviceIdType.MESH,
-        )
-    pl.semaphore_wait(barrier, CHIPS - 1)
+            barrier, inc=1, device_id={"dp": device}, device_id_type=pl.DeviceIdType.MESH
+        )
+    pl.semaphore_wait(barrier, len(partners))
+
+    line = []
+    if vector is not None:
+        line_send, line_recv, flat_send, flat_recv = scratch[3:7]
+        if vector == "gather":
+            own = small_out.at[spot, plane]
+            keep = pltpu.make_async_copy(small_in, own, local_sem.at[count])
+            keep.start()
+            start = small_in
+        else:
+            line_sum, flat_sum = scratch[7:9]
+            own = line_sum.at[plane]
+            own[...] = small_in[...]
+            start = own
+        for hop, device in enumerate(above):
+            line.append(remote(start, own, line_send.at[hop], line_recv.at[hop], device))
+            line[-1].start()
     copies = []
     for number, view in enumerate(views):
         for hop in (2, 1, 3):
             other = (chip + hop) % CHIPS
             source, target = view(sources[number], targets[number], other, chip)
-            copies.append(
-                pltpu.make_async_remote_copy(
-                    src_ref=source, dst_ref=target,
-                    send_sem=send_sem.at[number, hop], recv_sem=recv_sem.at[number, hop],
-                    device_id={"dp": base + other * CORES},
-                    device_id_type=pl.DeviceIdType.MESH,
-                )
-            )
+            copies.append(remote(source, target, send_sem.at[number, hop],
+                                 recv_sem.at[number, hop], base + other * CORES))
             copies[-1].start()
     for number, view in enumerate(views):
         source, target = view(sources[number], targets[number], chip, chip)
         copies.append(pltpu.make_async_copy(source, target, local_sem.at[number]))
         copies[-1].start()
+    if vector is not None:
+        for copy in line:
+            copy.wait()
+        if vector == "gather":
+            keep.wait()
+            block = small_out.at[spot]
+        else:
+            block = flat_sum.at[spot]
+            block[...] = functools.reduce(lambda x, y: x + y, [line_sum[i] for i in range(planes)])
+        for hop, device in enumerate(beside):
+            copies.append(remote(block, block, flat_send.at[hop], flat_recv.at[hop], device))
+            copies[-1].start()
     for copy in copies:
         copy.wait()
-
-
-def exchange(views, sources, shapes, collective_id):
+    if vector == "sum":
+        small_out[...] = functools.reduce(lambda x, y: x + y, [flat_sum[i] for i in range(PLANE)])
+
+
+def exchange(views, sources, shapes, collective_id, vector=None, small=None):
     count = len(views)
+    planes = lax.axis_size("dp") // PLANE
     moved = sum(math.prod(s.shape) * s.dtype.itemsize for s in shapes)
+    sources, shapes = list(sources), list(shapes)
+    specs = [pl.BlockSpec(memory_space=pl.ANY)] * count
+    dma = pltpu.SemaphoreType.DMA
+    scratch = [dma((count, CHIPS)), dma((count, CHIPS)), dma((count + 1,))]
+    if vector is not None:
+        sources.append(small)
+        scratch += [dma((planes,)), dma((planes,)), dma((PLANE,)), dma((PLANE,))]
+        if vector == "gather":
+            specs = specs + [pl.BlockSpec(memory_space=pl.ANY)]
+            shapes.append(jax.ShapeDtypeStruct((PLANE, planes) + small.shape, small.dtype))
+        else:
+            specs = specs + [pl.BlockSpec(memory_space=pltpu.VMEM)]
+            shapes.append(jax.ShapeDtypeStruct(small.shape, small.dtype))
+            scratch += [pltpu.VMEM((planes,) + small.shape, small.dtype),
+                        pltpu.VMEM((PLANE,) + small.shape, small.dtype)]
     return pl.pallas_call(
-        functools.partial(exchange_kernel, views, count),
-        out_shape=list(shapes),
-        in_specs=[pl.BlockSpec(memory_space=pl.ANY)] * count,
-        out_specs=[pl.BlockSpec(memory_space=pl.ANY)] * count,
-        scratch_shapes=[
-            pltpu.SemaphoreType.DMA((count, CHIPS)),
-            pltpu.SemaphoreType.DMA((count, CHIPS)),
-            pltpu.SemaphoreType.DMA((count,)),
-        ],
+        functools.partial(exchange_kernel, views, vector),
+        out_shape=shapes,
+        in_specs=specs,
+        out_specs=specs,
+        scratch_shapes=scratch,
         compiler_params=pltpu.CompilerParams(
             collective_id=collective_id, has_side_effects=True
         ),
         cost_estimate=pl.CostEstimate(flops=0, bytes_accessed=40 * moved, transcendentals=0),
     )(*sources)
+
+
+def to_arrival(info, x_ref, y_ref):
+    width = x_ref.shape[1] // 4
+    core = info[1]
+    x = [x_ref[:, i * width : (i + 1) * width] for i in range(4)]
+    for i, (zero, one) in enumerate(((0, 1), (2, 3), (1, 0), (3, 2))):
+        y_ref[:, i * width : (i + 1) * width] = jnp.where(core == 0, x[zero], x[one])
+
+
+def from_arrival(info, x_ref, y_ref):
+    width = x_ref.shape[1] // 4
+    core = info[1]
+    x = [x_ref[:, i * width : (i + 1) * width] for i in range(4)]
+    for i, (zero, one) in enumerate(((0, 2), (2, 0), (1, 3), (3, 1))):
+        y_ref[:, i * width : (i + 1) * width] = jnp.where(core == 0, x[zero], x[one])
+
+
+def finish_block(info, x_ref, adapter_ref, scale_ref, y_ref, base_ref):
+    from_arrival(info, x_ref, base_ref)
+    y_ref[...] = ((base_ref[...] + adapter_ref[...]) * scale_ref[...]).astype(y_ref.dtype)
+
+
+def reorder(kernel, arrays, kind, forward, info, planes, scratch=()):
+    rows, outputs = arrays[0].shape
+    block = outputs // planes // 2
+
+    def there(i, info):
+        number, side, plane = i // 2, i % 2, info[0]
+        falling = (plane + planes - number) % planes
+        rising = (plane + number) % planes if forward else (number + planes - plane) % planes
+        return 0, jnp.where(side == 0, falling, rising) * 2 + side
+
+    def here(i, info):
+        return 0, i
+
+    specs = [pl.BlockSpec((rows, block), there)]
+    specs += [pl.BlockSpec((a.shape[0], block), here) for a in arrays[1:]]
+    return pl.pallas_call(
+        kernel,
+        out_shape=jax.ShapeDtypeStruct((rows, outputs), kind),
+        grid_spec=pltpu.PrefetchScalarGridSpec(
+            num_scalar_prefetch=1,
+            grid=(planes * 2,),
+            in_specs=specs,
+            out_specs=pl.BlockSpec((rows, block), here),
+            scratch_shapes=list(scratch),
+        ),
+    )(info, *arrays)
 
 
 def rows_to_columns(depth):
@@ -126,17 +230,21 @@
     size = lax.axis_size("dp")
     planes = size // PLANE
     depth = features // CHIPS
-    half = outputs // planes // 2
+    block = outputs // planes
     me = lax.axis_index("dp")
     plane, chip, core = place()
+    info = jnp.stack([plane, core]).astype(jnp.int32)
     f32, bf16 = jnp.float32, jnp.bfloat16
 
-    (blocks,) = exchange(
+    own_up = lax.dynamic_slice_in_dim(up, me * width, width, 1)
+    combined = frozen.astype(f32) + jnp.dot(down, own_up, preferred_element_type=f32)
+    squares = jnp.broadcast_to(jnp.sum(combined * combined, axis=0)[None], (8, width))
+    blocks, squares = exchange(
         [frozen_view(depth, width)], [frozen],
-        [jax.ShapeDtypeStruct((2, depth, 2 * width), bf16)], 1,
-    )
-    blocks, tokens, frozen, cotangent = lax.optimization_barrier(
-        (blocks, tokens, frozen, cotangent)
+        [jax.ShapeDtypeStruct((2, depth, 2 * width), bf16)], 1, "gather", squares,
+    )
+    blocks, squares, tokens, cotangent = lax.optimization_barrier(
+        (blocks, squares, tokens, cotangent)
     )
 
     forward = [(i, (i + PLANE) % size) for i in range(size)]
@@ -151,16 +259,16 @@
     others = [[lax.ppermute(part, "dp", across) for part in pair] for pair in pieces]
 
     tokens_part, cotangent_part = exchange(
-        [rows_to_columns(depth), whole_rows], [tokens, cotangent],
+        [rows_to_columns(depth), whole_rows],
+        [tokens, reorder(to_arrival, [cotangent], bf16, True, info, planes)],
         [jax.ShapeDtypeStruct((CHIPS * rows, depth), bf16),
          jax.ShapeDtypeStruct((CHIPS * rows, outputs), bf16)], 2,
     )
 
-    own_up = lax.dynamic_slice_in_dim(up, me * width, width, 1)
-    combined = frozen.astype(f32) + jnp.dot(down, own_up, preferred_element_type=f32)
-    squares = lax.all_gather(jnp.sum(combined * combined, axis=0), "dp", axis=0, tiled=True)
-    norm = jnp.sqrt(squares + epsilon)
+    norm = jnp.sqrt(squares[:, :, 0, :].transpose(1, 0, 2).reshape(outputs) + epsilon)
     scale = magnitude.astype(f32) / norm
+    scale_rows = jnp.broadcast_to(scale[None], (8, outputs))
+    scale_arrival = reorder(to_arrival, [scale_rows], f32, True, info, planes)[:1]
 
     rank_act = jnp.dot(tokens, down, preferred_element_type=f32).astype(bf16)
     adapter = jnp.dot(rank_act, up, preferred_element_type=f32)
@@ -172,58 +280,46 @@
     up_part = dot(rank_act, grad_own, (0, 0))
     grad_down, grad_up = lax.psum((down_part, up_part), "dp")
 
-    grad_part = (cotangent_part.astype(f32) * scale).astype(bf16)
-    back_part = dot(grad_part, up, (1, 1)).astype(bf16)
+    grad_part = (cotangent_part.astype(f32) * scale_arrival).astype(bf16)
+    up_arrival = reorder(to_arrival, [up], bf16, True, info, planes)
+    back_part = dot(grad_part, up_arrival, (1, 1)).astype(bf16)
     down_rows = lax.dynamic_slice_in_dim(down, chip * depth, depth, 0)
     gradient = dot(back_part, down_rows, (1, 1))
 
     partial, sums = [], []
     for step in range(planes):
-        for side in range(2):
-            where = (plane + (planes - step if side == 0 else step)) % planes
-            start = where * 2 * half + side * half
-            group = (CHIPS * rows, 2, CORES, width)
-            cot = lax.dynamic_slice_in_dim(cotangent_part, start, half, 1)
-            grad = lax.dynamic_slice_in_dim(grad_part, start, half, 1).reshape(group)
-            outs = []
-            for part, kind in ((pieces[step][side], core), (others[step][side], 1 - core)):
-                outs.append(dot(tokens_part, part, (1, 0)))
-                grad_kind = lax.dynamic_index_in_dim(grad, kind, 2, False)
-                grad_kind = grad_kind.reshape(CHIPS * rows, 2 * width)
-                gradient = gradient + dot(grad_kind, part, (1, 1))
-            first = jnp.where(core == 0, outs[0], outs[1]).reshape(CHIPS * rows, 2, 1, width)
-            second = jnp.where(core == 0, outs[1], outs[0]).reshape(CHIPS * rows, 2, 1, width)
-            out = jnp.concatenate([first, second], axis=2).reshape(CHIPS * rows, half)
-            sums.append(jnp.sum(cot.astype(f32) * out, axis=0))
-            partial.append(out.astype(bf16))
-
-    early = jnp.concatenate(partial[:-2], axis=1)
-    late = jnp.concatenate(partial[-2:], axis=1)
+        weight = jnp.concatenate(
+            [pieces[step][0], others[step][0], pieces[step][1], others[step][1]], axis=1
+        )
+        columns = slice(step * block, (step + 1) * block)
+        out = dot(tokens_part, weight, (1, 0))
+        gradient = gradient + dot(grad_part[:, columns], weight, (1, 1))
+        if step < planes - 1:
+            gradient = lax.optimization_barrier(gradient)
+        sums.append(jnp.sum(cotangent_part[:, columns].astype(f32) * out, axis=0))
+        partial.append(out.astype(bf16))
+
+    early = jnp.concatenate(partial[:-1], axis=1)
+    late = partial[-1]
     (early_slots,) = exchange(
         [rows_to_slots(rows)], [early],
         [jax.ShapeDtypeStruct((CHIPS, rows, early.shape[1]), bf16)], 3,
     )
-    late_slots, input_gradient = exchange(
+    sums = jnp.broadcast_to(jnp.concatenate(sums)[None], (8, outputs))
+    sums = reorder(from_arrival, [sums], f32, False, info, planes)[0]
+    sums = (sums + jnp.sum(cot_own * adapter, axis=0)) / norm
+    late_slots, input_gradient, grad_magnitude = exchange(
         [rows_to_slots(rows), columns_to_rows(rows, depth)], [late, gradient.astype(bf16)],
-        [jax.ShapeDtypeStruct((CHIPS, rows, late.shape[1]), bf16),
+        [jax.ShapeDtypeStruct((CHIPS, rows, block), bf16),
          jax.ShapeDtypeStruct((rows, features), bf16)], 4,
-    )
-
-    def in_order(steps):
-        lead = steps.shape[:-1]
-        steps = steps.reshape(lead + (planes, 2, half))
-        number = jnp.arange(planes)
-        falling = jnp.take(steps[..., 0, :], (plane - number) % planes, axis=-2)
-        rising = jnp.take(steps[..., 1, :], (number - plane) % planes, axis=-2)
-        return jnp.stack([falling, rising], axis=-2).reshape(lead + (outputs,))
-
-    sums = in_order(jnp.concatenate(sums)) + jnp.sum(cot_own * adapter, axis=0)
-    grad_magnitude = jnp.sum(lax.all_gather(sums / norm, "dp"), axis=0)
-
+        "sum", sums.reshape(outputs // 128, 128),
+    )
+    grad_magnitude = grad_magnitude.reshape(outputs)
     base = jnp.concatenate(
         [jnp.sum(early_slots.astype(f32), axis=0), jnp.sum(late_slots.astype(f32), axis=0)], axis=1
     )
-    output = ((in_order(base) + adapter) * scale).astype(bf16)
+    output = reorder(finish_block, [base, adapter, scale[None]], bf16, False, info, planes,
+                     [pltpu.VMEM((rows, block // 2), f32)])
     return (output, input_gradient, grad_down * factor, grad_up * factor, grad_magnitude * factor)
 
 

time: 798 us -> 609 us (0.76)
  blocking collectives: 142 us -> 0 us
  matrix products: 207 us -> 94.1 us
  waiting for transfers between devices: 39 us -> 135 us
  local copies, waits for them, and re-layouts: 89.9 us -> 41.6 us
  Pallas kernels: 238 us -> 286 us
  other arithmetic: 49.3 us -> 21.7 us
    all_gather x2 -> x0, blocking collectives: 142 us -> none  [the longest x1 102 us: on_plane(): lax.all_gather(jnp.sum(combined * combined, axis=0), 'dp', axis=0, tiled=...]
    dot_general x35 -> x11, matrix products: 199 us -> 87.6 us  [dot(): lax.dot_general(a, b, ((contract[:1], contract[1:]), ((), ())), preferred...]
    psum x1, waiting for transfers between devices: 16.2 us -> 99.9 us  [on_plane(): grad_down, grad_up = lax.psum((down_part, up_part), 'dp')]
    pallas_call x4 -> x9, Pallas kernels: 238 us -> 286 us  [the longest x4 259 us: exchange(): pl.pallas_call(functools.partial(exchange_kernel, views, vector), out_sha...]
    reshape x26 -> x0, local copies, waits for them, and re-layouts: 37.6 us -> none  [the longest x8 21.2 us: on_plane(): out = jnp.concatenate([first, second], axis=2).reshape(CHIPS * rows, half)]
    dynamic_slice x13 -> x0, local copies, waits for them, and re-layouts: 24.3 us -> none  [the longest x9 17.8 us: on_plane(): grad = lax.dynamic_slice_in_dim(grad_part, start, half, 1).reshape(group)]
    unnamed x109 -> x45, local copies, waits for them, and re-layouts: 6.46 us -> 29 us
    concatenate x10 -> x2, other arithmetic: 16.3 us -> 2.82 us  [the longest x1 2.81 us: on_plane(): early = jnp.concatenate(partial[:-1], axis=1)]
  transfers between devices with their start and end apart: 15 -> 15, of which waited for: 3 -> 3; matrix products, arithmetic and copies ran while one was open for 31% -> 16% of each run, Pallas kernels for 18% -> 19%
where the time goes in v2:
time: 609 us; the launch traced here: 607 us
  Pallas kernels  286 us (47%)
  waiting for transfers between devices  135 us (22%)
  matrix products  94.1 us (15%)
  local copies, waits for them, and re-layouts  41.6 us (7%)
  other arithmetic  21.7 us (4%)
  between operations  14.3 us (2%)
  starting transfers between devices  13.6 us (2%)
    pallas_call x4, Pallas kernels, exchange(): pl.pallas_call(functools.partial(exchange_kernel, views, vector), out_sha...  259 us
    psum x1, waiting for transfers between devices, on_plane(): grad_down, grad_up = lax.psum((down_part, up_part), 'dp')  99.9 us
    dot_general x11, matrix products, dot(): lax.dot_general(a, b, ((contract[:1], contract[1:]), ((), ())), preferred...  87.6 us
    unnamed x45, local copies, waits for them, and re-layouts  29 us
    pallas_call x5, Pallas kernels, reorder(): pl.pallas_call(kernel, out_shape=jax.ShapeDtypeStruct((rows, outputs), ki...  27.7 us
    ppermute x3, waiting for transfers between devices, on_plane(): lax.ppermute(pieces[-1][1], 'dp', backward)  24.2 us
  transfers between devices with their start and end apart: 15, of which 3 were waited for; matrix products, arithmetic and copies ran while one was open for 16% of the time, Pallas kernels for 19%

profile of v2, /device:TPU:0, one launch (start us, length us, event | category | flops | bytes accessed | tf_op | source)
XLA Modules:
  0.0 606.9 jit_solution(14233348246671365155)
XLA Ops:
  7.2 6.2 %copy.13 = bf16[14336,128]{0,1:T(8,128)(2,1)} copy(bf16[14336,128]{1,0:T(8,128)(2,1)} %refs_0_.1) | data formatting | bytes 7340032 | tf_op args[1]
  17.4 48.8 %shard_map.101 = (bf16[2,3584,256]{2,1,0:T(8,128)(2,1)}, f32[8,4,8,128]{3,2,1,0:T(8,128)}) custom-call(bf16[14336,128]{1,0:T(8,128)(2,1)} %refs_0_.1, f32[8,128]{1,0:T(8,128)} %broadcast_in_dim.8.refs_1_), custom_call_target="tpu_custom_call" | custom-call | bytes 146800640 | tf_op jit(solution)/shard_map/pallas_call | solution.py:120
  75.2 5.5 fusion.7
  82.6 5.9 shard_map.102.refs_1_
  88.6 5.5 shard_map.106
  94.0 97.8 %shard_map.103 = (bf16[512,3584]{1,0:T(8,128)(2,1)}, bf16[512,4096]{1,0:T(8,128)(2,1)}) custom-call(bf16[128,14336]{1,0:T(8,128)(2,1)} %refs_0_.2, bf16[128,4096]{1,0:T(8,128)(2,1)} %shard_map.102.refs_1_), custom_call_target="tpu_custom_call" | custom-call | bytes 314572800 | tf_op jit(solution)/shard_map/pallas_call | solution.py:120
  192.5 4.8 shard_map.105
  198.3 5.2 multiply_convert_fusion
  203.5 9.4 %fusion.6 = f32[512,3584]{1,0:T(8,128)} fusion(bf16[512,4096]{1,0:T(8,128)(2,1)} %multiply_convert_fusion, bf16[64,4096]{1,0:T(8,128)(2,1)} %shard_map.106, bf16[14336,64]{0,1:T(8,128)(2,1)S(1)} %copy-done, s32[]{:T(128)S(6)} %select_n.29), kind=kOutput, calls=%fused_computation.27 | convolution fusion | flops 503349248 | bytes 12517380 | tf_op jit(solution)/shard_map/dot_general | solution.py:222
  214.7 9.6 %convolution_add_fusion.2 = f32[512,3584]{1,0:T(8,128)} fusion(f32[512,3584]{1,0:T(8,128)} %fusion.6, bf16[3584,256]{1,0:T(8,128)(2,1)} %collective-permute-done.1, bf16[3584,256]{1,0:T(8,128)(2,1)} %get-tuple-element.33, bf16[3584,256]{1,0:T(8,128)(2,1)} %collective-permute-done, bf16[3584,256]{1,0:T(8,128)(2,1)} %get-tuple-element.34, ...), kind=kOutput, calls=%fused_computation.9 | convolution fusion | flops 3789291520 | bytes 23068672 | tf_op jit(solution)/shard_map/dot_general | solution.py:222
  231.8 99.9 %all-reduce.3.cloned.1.call-done = (f32[14336,64]{0,1:T(8,128)}, f32[64,4096]{1,0:T(8,128)}) async-done(((f32[14336,64]{0,1:T(8,128)}, f32[64,4096]{1,0:T(8,128)}), (f32[14336,64]{0,1:T(8,128)}, f32[64,4096]{1,0:T(8,128)})) %all-reduce.3.cloned.1.call-update) | async-done | bytes 4718608 | tf_op jit(solution)/shard_map/psum | solution.py:281
  347.9 10.2 %convolution_add_fusion.1 = f32[512,3584]{1,0:T(8,128)} fusion(f32[512,3584]{1,0:T(8,128)} %convolution_add_fusion.2, bf16[3584,1024]{1,0:T(8,128)(2,1)} %constant_dynamic-update-slice_fusion, bf16[512,4096]{1,0:T(8,128)(2,1)S(1)} %copy-done.5), kind=kOutput, calls=%fused_computation.8 | convolution fusion | flops 3759931392 | bytes 23068672 | tf_op jit(solution)/shard_map/dot_general | solution.py:222
  365.7 7.7 %fusion.22 = f32[512,1024]{1,0:T(8,128)} fusion(bf16[512,3584]{1,0:T(8,128)(2,1)S(1)} %copy-done.13, bf16[3584,1024]{1,0:T(8,128)(2,1)} %constant_dynamic-update-slice_fusion), kind=kOutput, calls=%fused_computation.62 | convolution fusion | flops 3758096384 | bytes 13107200 | tf_op jit(solution)/shard_map/dot_general | solution.py:222
  373.4 11.1 %collective-permute-done.10 = bf16[3584,256]{1,0:T(8,128)(2,1)S(1)} collective-permute-done((bf16[3584,256]{1,0:T(8,128)(2,1)}, bf16[3584,256]{1,0:T(8,128)(2,1)S(1)}, u32[]{:S(2)}, u32[]{:S(2)}) %collective-permute-start.10) | collective-permute-done | bytes 1835040 | tf_op jit(solution)/shard_map/ppermute | solution.py:256
  388.8 10.2 %convolution_add_fusion = f32[512,3584]{1,0:T(8,128)} fusion(f32[512,3584]{1,0:T(8,128)} %convolution_add_fusion.1, bf16[3584,1024]{1,0:T(8,128)(2,1)} %constant_dynamic-update-slice_fusion.4, bf16[512,4096]{1,0:T(8,128)(2,1)S(1)} %copy-done.5), kind=kOutput, calls=%fused_computation.7 | convolution fusion | flops 3759931392 | bytes 23068672 | tf_op jit(solution)/shard_map/dot_general | solution.py:222
  399.0 24.2 %collective-permute-done.12 = bf16[3584,256]{1,0:T(8,128)(2,1)S(1)} collective-permute-done((bf16[3584,256]{1,0:T(8,128)(2,1)S(1)}, bf16[3584,256]{1,0:T(8,128)(2,1)S(1)}, u32[]{:S(2)}, u32[]{:S(2)}) %collective-permute-start.12) | collective-permute-done | bytes 1835040 | tf_op jit(solution)/shard_map/ppermute | solution.py:257
  423.5 7.6 %fusion.23 = f32[512,1024]{1,0:T(8,128)} fusion(bf16[512,3584]{1,0:T(8,128)(2,1)S(1)} %copy-done.14, bf16[3584,1024]{1,0:T(8,128)(2,1)} %constant_dynamic-update-slice_fusion.4), kind=kOutput, calls=%fused_computation.63 | convolution fusion | flops 3758096384 | bytes 13107200 | tf_op jit(solution)/shard_map/dot_general | solution.py:222
  434.9 5.3 fusion.24
  440.2 9.8 %add_convert_fusion.refs_1_ = bf16[512,3584]{1,0:T(8,128)(2,1)} fusion(f32[512,3584]{1,0:T(8,128)} %convolution_add_fusion, bf16[3584,1024]{1,0:T(8,128)(2,1)} %copy-done.9, bf16[512,4096]{1,0:T(8,128)(2,1)S(1)} %copy-done.5), kind=kOutput, calls=%fused_computation.5 | convolution fusion | flops 3761766400 | bytes 19398656 | tf_op jit(solution)/shard_map/dot_general | solution.py:222
  450.0 11.1 %multiply_reduce_fusion.3 = (f32[1024]{0:T(1024)S(1)}, f32[1024]{0:T(1024)S(1)}, f32[1024]{0:T(1024)S(1)}, f32[1024]{0:T(1024)S(1)}, bf16[512,1024]{1,0:T(8,128)...) fusion(bf16[512,4096]{1,0:T(8,128)(2,1)} %get-tuple-element.22, ...), kind=kOutput, calls=%fused_computation.20 | convolution fusion | flops 3795841024 | bytes 25706496 | tf_op jit(solution)/shard_map/dot_general | solution.py:222
  461.8 4.8 shard_map.107
  468.2 73.9 %shard_map.108 = (bf16[4,128,1024]{2,1,0:T(8,128)(2,1)}, bf16[128,14336]{1,0:T(8,128)(2,1)}, f32[32,128]{1,0:T(8,128)}) custom-call(bf16[512,1024]{1,0:T(8,128)(2,1)} %get-tuple-element.38.refs_0_, bf16[512,3584]{1,0:T(8,128)(2,1)} %add_convert_fusion.refs_1_, f32[32,128]{1,0:T(8,128)} %bitcast_multiply_fusion.refs_2_), custom_call_target="tpu_custom_call" | custom-call | bytes 188743680 | tf_op jit(solution)/shard_map/pallas_call | solution.py:120
  546.3 38.2 %shard_map.104 = bf16[4,128,3072]{2,1,0:T(8,128)(2,1)} custom-call(bf16[512,3072]{1,0:T(8,128)(2,1)} %pad_maximum_fusion.1.refs_0_), custom_call_target="tpu_custom_call" | custom-call | bytes 125829120 | tf_op jit(solution)/shard_map/pallas_call | solution.py:120
  589.2 6.7 %shard_map.109 = bf16[128,4096]{1,0:T(8,128)(2,1)} custom-call(s32[2]{0:T(128)} %pad_add_fusion.info, f32[128,4096]{1,0:T(8,128)} %pad_maximum_fusion.2.x_ref, f32[128,4096]{1,0:T(8,128)} %get-tuple-element.41.adapter_ref, f32[1,4096]{1,0:T(1,128)} %bitcast.50), custom_call_target="tpu_custom_call" | custom-call | tf_op jit(solution)/shard_map/pallas_call | solution.py:169
  (97 shorter events, 73.3 us)
Async XLA Ops:
  7.2 324.6 %all-reduce.3.cloned.1.call-start = ((), (), s32[]{:S(2)}) async-start(), calls=%async_computation | async-start | bytes 9437184 | tf_op jit(solution)/shard_map/psum | solution.py:281
  66.2 7.5 %copy-start.2 = (bf16[128,14336]{1,0:T(8,128)(2,1)S(1)}, bf16[128,14336]{1,0:T(8,128)(2,1)}, u32[]{:S(2)}) copy-start(bf16[128,14336]{1,0:T(8,128)(2,1)} %refs_0_.2) | copy-start | bytes 11010052
  70.6 154.4 %collective-permute-start.4 = (bf16[3584,256]{1,0:T(8,128)(2,1)}, bf16[3584,256]{1,0:T(8,128)(2,1)}, u32[]{:S(2)}, u32[]{:S(2)}) collective-permute-start(bf16[3584,256]{1,0:T(8,128)(2,1)} %get-tuple-element.33), channel_id=1, source_target_pairs={{8,0},{9,1},{10,2},{11,3},{12,4},{13,5},{14,6},{15,7},{16,8},{17,9... | collective-permute-start | bytes 5505032 | tf_op jit(solution)/shard_map/ppermute | solution.py:257
  72.1 142.6 %collective-permute-start.1 = (bf16[3584,256]{1,0:T(8,128)(2,1)}, bf16[3584,256]{1,0:T(8,128)(2,1)}, u32[]{:S(2)}, u32[]{:S(2)}) collective-permute-start(bf16[3584,256]{1,0:T(8,128)(2,1)} %get-tuple-element.33), channel_id=1, source_target_pairs={{0,1},{1,0},{2,3},{3,2},{4,5},{5,4},{6,7},{7,6},{8,9},{9,8},{10,11... | collective-permute-start | bytes 5505032 | tf_op jit(solution)/shard_map/ppermute | solution.py:259
  72.1 152.2 %collective-permute-start.2 = (bf16[3584,256]{1,0:T(8,128)(2,1)}, bf16[3584,256]{1,0:T(8,128)(2,1)}, u32[]{:S(2)}, u32[]{:S(2)}) collective-permute-start(bf16[3584,256]{1,0:T(8,128)(2,1)} %get-tuple-element.34), channel_id=1, source_target_pairs={{0,8},{1,9},{2,10},{3,11},{4,12},{5,13},{6,14},{7,15},{8,16},{9,17... | collective-permute-start | bytes 5505032 | tf_op jit(solution)/shard_map/ppermute | solution.py:256
  72.6 142.1 %collective-permute-start = (bf16[3584,256]{1,0:T(8,128)(2,1)}, bf16[3584,256]{1,0:T(8,128)(2,1)}, u32[]{:S(2)}, u32[]{:S(2)}) collective-permute-start(bf16[3584,256]{1,0:T(8,128)(2,1)} %get-tuple-element.34), channel_id=1, source_target_pairs={{0,1},{1,0},{2,3},{3,2},{4,5},{5,4},{6,7},{7,6},{8,9},{9,8},{10,11... | collective-permute-start | bytes 5505032 | tf_op jit(solution)/shard_map/ppermute | solution.py:259
  75.2 116.7 %copy-start.10 = (f32[4096]{0:T(1024)}, f32[4096]{0:T(1024)S(1)}, u32[]{:S(2)}) copy-start(f32[4096]{0:T(1024)S(1)} %bitcast_multiply_fusion.1) | copy-start | bytes 49156
  203.5 9.4 %copy-start.4 = (bf16[128,4096]{1,0:T(8,128)(2,1)S(1)}, bf16[128,4096]{1,0:T(8,128)(2,1)}, u32[]{:S(2)}) copy-start(bf16[128,4096]{1,0:T(8,128)(2,1)} %x_ref.1) | copy-start | bytes 3145732
  203.5 9.4 %copy-start.7 = (bf16[64,4096]{1,0:T(8,128)(2,1)S(1)}, bf16[64,4096]{1,0:T(8,128)(2,1)}, u32[]{:S(2)}) copy-start(bf16[64,4096]{1,0:T(8,128)(2,1)} %x_ref.2) | copy-start | bytes 1572868
  224.3 112.7 %collective-permute-start.6 = (bf16[3584,256]{1,0:T(8,128)(2,1)}, bf16[3584,256]{1,0:T(8,128)(2,1)}, u32[]{:S(2)}, u32[]{:S(2)}) collective-permute-start(bf16[3584,256]{1,0:T(8,128)(2,1)} %collective-permute-done.2), channel_id=1, source_target_pairs={{0,8},{1,9},{2,10},{3,11},{4,12},{5,13},{6,14},{7,15},{8,16},{9,17... | collective-permute-start | bytes 5505032 | tf_op jit(solution)/shard_map/ppermute | solution.py:256
  225.0 114.0 %collective-permute-start.3 = (bf16[3584,256]{1,0:T(8,128)(2,1)}, bf16[3584,256]{1,0:T(8,128)(2,1)}, u32[]{:S(2)}, u32[]{:S(2)}) collective-permute-start(bf16[3584,256]{1,0:T(8,128)(2,1)} %collective-permute-done.2), channel_id=1, source_target_pairs={{0,1},{1,0},{2,3},{3,2},{4,5},{5,4},{6,7},{7,6},{8,9},{9,8},{10,11... | collective-permute-start | bytes 5505032 | tf_op jit(solution)/shard_map/ppermute | solution.py:259
  225.0 133.1 %collective-permute-start.8 = (bf16[3584,256]{1,0:T(8,128)(2,1)}, bf16[3584,256]{1,0:T(8,128)(2,1)S(1)}, u32[]{:S(2)}, u32[]{:S(2)}) collective-permute-start(bf16[3584,256]{1,0:T(8,128)(2,1)} %collective-permute-done.4), channel_id=1, source_target_pairs={{8,0},{9,1},{10,2},{11,3},{12,4},{13,5},{14,6},{15,7},{16,8},{17,9... | collective-permute-start | bytes 5505032 | tf_op jit(solution)/shard_map/ppermute | solution.py:257
  228.9 116.2 %collective-permute-start.5 = (bf16[3584,256]{1,0:T(8,128)(2,1)}, bf16[3584,256]{1,0:T(8,128)(2,1)}, u32[]{:S(2)}, u32[]{:S(2)}) collective-permute-start(bf16[3584,256]{1,0:T(8,128)(2,1)} %collective-permute-done.4), channel_id=1, source_target_pairs={{0,1},{1,0},{2,3},{3,2},{4,5},{5,4},{6,7},{7,6},{8,9},{9,8},{10,11... | collective-permute-start | bytes 5505032 | tf_op jit(solution)/shard_map/ppermute | solution.py:259
  337.0 47.5 %collective-permute-start.10 = (bf16[3584,256]{1,0:T(8,128)(2,1)}, bf16[3584,256]{1,0:T(8,128)(2,1)S(1)}, u32[]{:S(2)}, u32[]{:S(2)}) collective-permute-start(bf16[3584,256]{1,0:T(8,128)(2,1)} %collective-permute-done.6), channel_id=1, source_target_pairs={{0,8},{1,9},{2,10},{3,11},{4,12},{5,13},{6,14},{7,15},{8,16},{9,17... | collective-permute-start | bytes 5505032 | tf_op jit(solution)/shard_map/ppermute | solution.py:256
  339.0 45.6 %collective-permute-start.7 = (bf16[3584,256]{1,0:T(8,128)(2,1)}, bf16[3584,256]{1,0:T(8,128)(2,1)S(1)}, u32[]{:S(2)}, u32[]{:S(2)}) collective-permute-start(bf16[3584,256]{1,0:T(8,128)(2,1)} %collective-permute-done.6), channel_id=1, source_target_pairs={{0,1},{1,0},{2,3},{3,2},{4,5},{5,4},{6,7},{7,6},{8,9},{9,8},{10,11... | collective-permute-start | bytes 5505032 | tf_op jit(solution)/shard_map/ppermute | solution.py:259
  358.1 7.6 %copy-start.13 = (bf16[512,3584]{1,0:T(8,128)(2,1)S(1)}, bf16[512,3584]{1,0:T(8,128)(2,1)}, u32[]{:S(2)}) copy-start(bf16[512,3584]{1,0:T(8,128)(2,1)} %get-tuple-element.20) | copy-start | bytes 11010052
  358.1 65.0 %collective-permute-start.12 = (bf16[3584,256]{1,0:T(8,128)(2,1)S(1)}, bf16[3584,256]{1,0:T(8,128)(2,1)S(1)}, u32[]{:S(2)}, u32[]{:S(2)}) collective-permute-start(bf16[3584,256]{1,0:T(8,128)(2,1)S(1)} %collective-permute-done.8), channel_id=1, source_target_pairs={{8,0},{9,1},{10,2},{11,3},{12,4},{13,5},{14,6},{15,7},{16,8},{17,9... | collective-permute-start | bytes 5505032 | tf_op jit(solution)/shard_map/ppermute | solution.py:257
  362.6 24.8 %collective-permute-start.9 = (bf16[3584,256]{1,0:T(8,128)(2,1)S(1)}, bf16[3584,256]{1,0:T(8,128)(2,1)S(1)}, u32[]{:S(2)}, u32[]{:S(2)}) collective-permute-start(bf16[3584,256]{1,0:T(8,128)(2,1)S(1)} %collective-permute-done.8), channel_id=1, source_target_pairs={{0,1},{1,0},{2,3},{3,2},{4,5},{5,4},{6,7},{7,6},{8,9},{9,8},{10,11... | collective-permute-start | bytes 5505032 | tf_op jit(solution)/shard_map/ppermute | solution.py:259
  384.5 46.6 %collective-permute-start.11 = (bf16[3584,256]{1,0:T(8,128)(2,1)S(1)}, bf16[3584,256]{1,0:T(8,128)(2,1)S(1)}, u32[]{:S(2)}, u32[]{:S(2)}) collective-permute-start(bf16[3584,256]{1,0:T(8,128)(2,1)S(1)} %collective-permute-done.10), channel_id=1, source_target_pairs={{0,1},{1,0},{2,3},{3,2},{4,5},{5,4},{6,7},{7,6},{8,9},{9,8},{10,11... | collective-permute-start | bytes 5505032 | tf_op jit(solution)/shard_map/ppermute | solution.py:259
  399.0 24.6 %copy-start.14 = (bf16[512,3584]{1,0:T(8,128)(2,1)S(1)}, bf16[512,3584]{1,0:T(8,128)(2,1)}, u32[]{:S(2)}) copy-start(bf16[512,3584]{1,0:T(8,128)(2,1)} %get-tuple-element.20) | copy-start | bytes 11010052
  423.2 8.4 %collective-permute-start.13 = (bf16[3584,256]{1,0:T(8,128)(2,1)S(1)}, bf16[3584,256]{1,0:T(8,128)(2,1)S(1)}, u32[]{:S(2)}, u32[]{:S(2)}) collective-permute-start(bf16[3584,256]{1,0:T(8,128)(2,1)S(1)} %collective-permute-done.12), channel_id=1, source_target_pairs={{0,1},{1,0},{2,3},{3,2},{4,5},{5,4},{6,7},{7,6},{8,9},{9,8},{10,11... | collective-permute-start | bytes 5505032 | tf_op jit(solution)/shard_map/ppermute | solution.py:259
  440.2 9.8 %copy-start.15 = (bf16[512,3584]{1,0:T(8,128)(2,1)S(1)}, bf16[512,3584]{1,0:T(8,128)(2,1)}, u32[]{:S(2)}) copy-start(bf16[512,3584]{1,0:T(8,128)(2,1)} %get-tuple-element.20) | copy-start | bytes 11010052
  440.2 9.8 %copy-start.16 = (f32[512,1024]{1,0:T(8,128)S(1)}, f32[512,1024]{1,0:T(8,128)}, u32[]{:S(2)}) copy-start(f32[512,1024]{1,0:T(8,128)} %fusion.22) | copy-start | bytes 6291460
  589.2 10.9 %copy-start.1 = (bf16[14336,64]{0,1:T(8,128)(2,1)S(1)}, bf16[14336,64]{0,1:T(8,128)(2,1)}, u32[]{:S(2)}) copy-start(bf16[14336,64]{0,1:T(8,128)(2,1)} %param.8) | copy-start | bytes 5505028
  (8 other events, 37.7 us)
Sparse Core Ops, SparseCore 0:
  82.1 249.5 all-reduce.2

commit v3 on v2

--- a/solution.py
+++ b/solution.py
@@ -23,8 +23,11 @@
 def exchange_kernel(views, vector, *refs):
     count = len(views)
     ends = count + (vector is not None)
+    if vector == "sum":
+        ends += 1
     sources, targets = refs[:count], refs[ends : ends + count]
-    small_in, small_out = refs[ends - 1], refs[2 * ends - 1]
+    small_in, small_out = refs[count], refs[ends + count]
+    terms, totals = refs[ends - 1], refs[2 * ends - 1]
     scratch = refs[2 * ends :]
     send_sem, recv_sem, local_sem = scratch[:3]
     me = lax.axis_index("dp")
@@ -32,6 +35,7 @@
     plane, chip, core = place()
     spot = me % PLANE
     base = me - chip * CORES
+    sibling = me - core + (core + 1) % CORES
 
     def remote(source, target, send, recv, device):
         return pltpu.make_async_remote_copy(
@@ -45,6 +49,15 @@
         above = [(plane + hop) % planes * PLANE + spot for hop in range(1, planes)]
         beside = [plane * PLANE + (spot + hop) % PLANE for hop in range(1, PLANE)]
         partners = above + beside
+        group = {}
+        for turn in range(CORES):
+            for hop in range(planes):
+                if turn + hop > 0:
+                    group[turn, hop] = (
+                        (plane + hop) % planes * PLANE + chip * CORES + (core + turn) % CORES
+                    )
+        if vector == "sum":
+            partners = partners + [group[1, hop] for hop in range(1, planes)]
     barrier = pltpu.get_barrier_semaphore()
     for device in partners:
         pl.semaphore_signal(
@@ -61,7 +74,16 @@
             keep.start()
             start = small_in
         else:
-            line_sum, flat_sum = scratch[7:9]
+            line_sum, flat_sum, parts, total, part_send, part_recv, total_send, total_recv = scratch[7:]
+            mine = parts.at[core, plane]
+            keep = pltpu.make_async_copy(terms.at[core, plane], mine, local_sem.at[count])
+            keep.start()
+            shares = []
+            for (turn, hop), device in group.items():
+                theirs = terms.at[(core + turn) % CORES, (plane + hop) % planes]
+                shares.append(remote(theirs, mine, part_send.at[turn, hop],
+                                     part_recv.at[turn, hop], device))
+                shares[-1].start()
             own = line_sum.at[plane]
             own[...] = small_in[...]
             start = own
@@ -92,13 +114,40 @@
         for hop, device in enumerate(beside):
             copies.append(remote(block, block, flat_send.at[hop], flat_recv.at[hop], device))
             copies[-1].start()
+    if vector == "sum":
+        for copy in shares:
+            copy.wait()
+        keep.wait()
+        total[...] = functools.reduce(
+            lambda x, y: x + y, [parts[k, z] for k in range(CORES) for z in range(planes)]
+        )
+        place_of = totals.at[core, chip, plane]
+        keep = pltpu.make_async_copy(total, place_of, local_sem.at[count])
+        keep.start()
+        stage = [remote(total, place_of, total_send.at[0, hop], total_recv.at[0, hop], device)
+                 for hop, device in enumerate(above)]
+        for copy in stage:
+            copy.start()
+        for copy in stage:
+            copy.wait()
+        keep.wait()
+        column = totals.at[core, chip]
+        stage = [remote(column, column, total_send.at[1, hop], total_recv.at[1, hop],
+                        base + ((chip + hop) % CHIPS) * CORES) for hop in range(1, CHIPS)]
+        for copy in stage:
+            copy.start()
+        for copy in stage:
+            copy.wait()
+        side = totals.at[core]
+        copies.append(remote(side, side, total_send.at[2, 0], total_recv.at[2, 0], sibling))
+        copies[-1].start()
     for copy in copies:
         copy.wait()
     if vector == "sum":
         small_out[...] = functools.reduce(lambda x, y: x + y, [flat_sum[i] for i in range(PLANE)])
 
 
-def exchange(views, sources, shapes, collective_id, vector=None, small=None):
+def exchange(views, sources, shapes, collective_id, vector=None, small=None, terms=None):
     count = len(views)
     planes = lax.axis_size("dp") // PLANE
     moved = sum(math.prod(s.shape) * s.dtype.itemsize for s in shapes)
@@ -117,6 +166,12 @@
             shapes.append(jax.ShapeDtypeStruct(small.shape, small.dtype))
             scratch += [pltpu.VMEM((planes,) + small.shape, small.dtype),
                         pltpu.VMEM((PLANE,) + small.shape, small.dtype)]
+            sources.append(terms)
+            specs = specs + [pl.BlockSpec(memory_space=pl.ANY)]
+            piece = terms.shape[2:]
+            shapes.append(jax.ShapeDtypeStruct((CORES, CHIPS, planes) + piece, terms.dtype))
+            scratch += [pltpu.VMEM(terms.shape, terms.dtype), pltpu.VMEM(piece, terms.dtype),
+                        dma((CORES, planes)), dma((CORES, planes)), dma((3, 4)), dma((3, 4))]
     return pl.pallas_call(
         functools.partial(exchange_kernel, views, vector),
         out_shape=shapes,
@@ -128,6 +183,96 @@
         ),
         cost_estimate=pl.CostEstimate(flops=0, bytes_accessed=40 * moved, transcendentals=0),
     )(*sources)
+
+
+def ring_kernel(views, steps, *refs):
+    count = len(views)
+    blocks, sources = refs[0], refs[1 : 1 + count]
+    weights, refs = refs[1 + count : 2 + count + steps], refs[2 + count + steps :]
+    targets = refs[:count]
+    send_sem, recv_sem, ring_send, ring_recv, side_send, side_recv, local_sem = refs[count:]
+    me = lax.axis_index("dp")
+    size = lax.axis_size("dp")
+    plane, chip, core = place()
+    base = me - chip * CORES
+    sibling = me - core + (core + 1) % CORES
+    after, before = (me + PLANE) % size, (me + size - PLANE) % size
+    width = blocks.shape[2]
+
+    def remote(source, target, send, recv, device):
+        return pltpu.make_async_remote_copy(
+            src_ref=source, dst_ref=target, send_sem=send, recv_sem=recv,
+            device_id={"dp": device}, device_id_type=pl.DeviceIdType.MESH,
+        )
+
+    partners = [base + ((chip + hop) % CHIPS) * CORES for hop in range(1, CHIPS)]
+    partners += [sibling, after, before]
+    barrier = pltpu.get_barrier_semaphore()
+    for device in partners:
+        pl.semaphore_signal(
+            barrier, inc=1, device_id={"dp": device}, device_id_type=pl.DeviceIdType.MESH
+        )
+    pl.semaphore_wait(barrier, len(partners))
+
+    def spot(step, side, other):
+        return weights[step].at[:, pl.ds((side * 2 + other) * width, width)]
+
+    def send(step):
+        ring, across = [], []
+        for side, device in enumerate((after, before)):
+            source = blocks.at[side] if step == 0 else spot(step, side, 0)
+            if step < steps:
+                ring.append(remote(source, spot(step + 1, side, 0), ring_send.at[step, side],
+                                   ring_recv.at[step, side], device))
+                ring[-1].start()
+            across.append(remote(source, spot(step, side, 1), side_send.at[step, side],
+                                 side_recv.at[step, side], sibling))
+            across[-1].start()
+        return ring, across
+
+    ring, copies = send(0)
+    for number, view in enumerate(views):
+        for hop in (2, 1, 3):
+            other = (chip + hop) % CHIPS
+            source, target = view(sources[number], targets[number], other, chip)
+            copies.append(remote(source, target, send_sem.at[number, hop],
+                                 recv_sem.at[number, hop], base + other * CORES))
+            copies[-1].start()
+    for number, view in enumerate(views):
+        source, target = view(sources[number], targets[number], chip, chip)
+        copies.append(pltpu.make_async_copy(source, target, local_sem.at[number]))
+        copies[-1].start()
+    for side in range(2):
+        copies.append(pltpu.make_async_copy(
+            blocks.at[side], spot(0, side, 0), local_sem.at[count + side]))
+        copies[-1].start()
+    for step in range(1, steps + 1):
+        for copy in ring:
+            copy.wait()
+        ring, across = send(step)
+        copies += across
+    for copy in copies:
+        copy.wait()
+
+
+def ring_exchange(blocks, steps, views, sources, shapes, collective_id):
+    count = len(views)
+    _, depth, width = blocks.shape
+    dma = pltpu.SemaphoreType.DMA
+    anywhere = pl.BlockSpec(memory_space=pl.ANY)
+    return pl.pallas_call(
+        functools.partial(ring_kernel, views, steps),
+        out_shape=[jax.ShapeDtypeStruct((depth, 4 * width), blocks.dtype)] * (steps + 1) + list(shapes),
+        in_specs=[anywhere] * (count + 1),
+        out_specs=[anywhere] * (count + steps + 1),
+        scratch_shapes=[dma((count, CHIPS)), dma((count, CHIPS)),
+                        dma((steps + 1, 2)), dma((steps + 1, 2)),
+                        dma((steps + 1, 2)), dma((steps + 1, 2)), dma((count + 2,))],
+        compiler_params=pltpu.CompilerParams(
+            collective_id=collective_id, has_side_effects=True
+        ),
+        cost_estimate=pl.CostEstimate(flops=0, bytes_accessed=400_000_000, transcendentals=0),
+    )(blocks, *sources)
 
 
 def to_arrival(info, x_ref, y_ref):
@@ -243,26 +388,25 @@
         [frozen_view(depth, width)], [frozen],
         [jax.ShapeDtypeStruct((2, depth, 2 * width), bf16)], 1, "gather", squares,
     )
-    blocks, squares, tokens, cotangent = lax.optimization_barrier(
-        (blocks, squares, tokens, cotangent)
+    rank_act = jnp.dot(tokens, down, preferred_element_type=f32).astype(bf16)
+    steps = planes - 2
+    *weights, tokens_part, cotangent_part, rank_part = ring_exchange(
+        blocks, steps, [rows_to_columns(depth), whole_rows, whole_rows],
+        [tokens, reorder(to_arrival, [cotangent], bf16, True, info, planes),
+         jnp.pad(rank_act, ((0, 0), (0, 128 - rank_act.shape[1] % 128)))],
+        [jax.ShapeDtypeStruct((CHIPS * rows, depth), bf16),
+         jax.ShapeDtypeStruct((CHIPS * rows, outputs), bf16),
+         jax.ShapeDtypeStruct((CHIPS * rows, 128), bf16)], 2,
     )
 
     forward = [(i, (i + PLANE) % size) for i in range(size)]
     backward = [((i + PLANE) % size, i) for i in range(size)]
     across = [(i, i - i % CORES + (i + 1) % CORES) for i in range(size)]
-    pieces = [[blocks[0], blocks[1]]]
-    for step in range(planes - 1):
-        pieces.append([
-            lax.ppermute(pieces[-1][0], "dp", forward),
-            lax.ppermute(pieces[-1][1], "dp", backward),
-        ])
-    others = [[lax.ppermute(part, "dp", across) for part in pair] for pair in pieces]
-
-    tokens_part, cotangent_part = exchange(
-        [rows_to_columns(depth), whole_rows],
-        [tokens, reorder(to_arrival, [cotangent], bf16, True, info, planes)],
-        [jax.ShapeDtypeStruct((CHIPS * rows, depth), bf16),
-         jax.ShapeDtypeStruct((CHIPS * rows, outputs), bf16)], 2,
+    falling = lax.ppermute(weights[steps][:, : 2 * width], "dp", forward)
+    rising = lax.ppermute(weights[steps][:, 4 * width : 6 * width], "dp", backward)
+    last = jnp.concatenate(
+        [falling, lax.ppermute(falling, "dp", across), rising, lax.ppermute(rising, "dp", across)],
+        axis=1,
     )
 
     norm = jnp.sqrt(squares[:, :, 0, :].transpose(1, 0, 2).reshape(outputs) + epsilon)
@@ -270,15 +414,9 @@
     scale_rows = jnp.broadcast_to(scale[None], (8, outputs))
     scale_arrival = reorder(to_arrival, [scale_rows], f32, True, info, planes)[:1]
 
-    rank_act = jnp.dot(tokens, down, preferred_element_type=f32).astype(bf16)
     adapter = jnp.dot(rank_act, up, preferred_element_type=f32)
     cot_own = cotangent.astype(f32)
-    grad_own = (cot_own * scale).astype(bf16)
-    back_own = dot(grad_own, up, (1, 1)).astype(bf16)
     factor = 1.0 / math.sqrt(rows * size)
-    down_part = dot(tokens, back_own, (0, 0))
-    up_part = dot(rank_act, grad_own, (0, 0))
-    grad_down, grad_up = lax.psum((down_part, up_part), "dp")
 
     grad_part = (cotangent_part.astype(f32) * scale_arrival).astype(bf16)
     up_arrival = reorder(to_arrival, [up], bf16, True, info, planes)
@@ -286,11 +424,17 @@
     down_rows = lax.dynamic_slice_in_dim(down, chip * depth, depth, 0)
     gradient = dot(back_part, down_rows, (1, 1))
 
+    rank = up.shape[0]
+    down_part = dot(back_part, tokens_part, (0, 0))
+    up_part = dot(rank_part, grad_part, (0, 0))[:rank]
+    up_part = reorder(from_arrival, [up_part], f32, False, info, planes)
+    up_part = lax.dynamic_slice_in_dim(up_part, chip * (outputs // CHIPS), outputs // CHIPS, 1)
+    terms = jnp.concatenate([down_part, up_part], axis=1)
+    terms = terms.reshape(CORES, planes, rank // (CORES * planes), terms.shape[1])
+
     partial, sums = [], []
     for step in range(planes):
-        weight = jnp.concatenate(
-            [pieces[step][0], others[step][0], pieces[step][1], others[step][1]], axis=1
-        )
+        weight = weights[step] if step <= steps else last
         columns = slice(step * block, (step + 1) * block)
         out = dot(tokens_part, weight, (1, 0))
         gradient = gradient + dot(grad_part[:, columns], weight, (1, 1))
@@ -308,19 +452,23 @@
     sums = jnp.broadcast_to(jnp.concatenate(sums)[None], (8, outputs))
     sums = reorder(from_arrival, [sums], f32, False, info, planes)[0]
     sums = (sums + jnp.sum(cot_own * adapter, axis=0)) / norm
-    late_slots, input_gradient, grad_magnitude = exchange(
+    early_slots, late, sums = lax.optimization_barrier((early_slots, late, sums))
+    late_slots, input_gradient, grad_magnitude, totals = exchange(
         [rows_to_slots(rows), columns_to_rows(rows, depth)], [late, gradient.astype(bf16)],
         [jax.ShapeDtypeStruct((CHIPS, rows, block), bf16),
          jax.ShapeDtypeStruct((rows, features), bf16)], 4,
-        "sum", sums.reshape(outputs // 128, 128),
-    )
+        "sum", sums.reshape(outputs // 128, 128), terms,
+    )
+    totals = totals.transpose(0, 2, 3, 1, 4) * factor
+    grad_down = totals[..., :depth].reshape(rank, features).T
+    grad_up = totals[..., depth:].reshape(rank, outputs)
     grad_magnitude = grad_magnitude.reshape(outputs)
     base = jnp.concatenate(
         [jnp.sum(early_slots.astype(f32), axis=0), jnp.sum(late_slots.astype(f32), axis=0)], axis=1
     )
     output = reorder(finish_block, [base, adapter, scale[None]], bf16, False, info, planes,
                      [pltpu.VMEM((rows, block // 2), f32)])
-    return (output, input_gradient, grad_down * factor, grad_up * factor, grad_magnitude * factor)
+    return (output, input_gradient, grad_down, grad_up, grad_magnitude * factor)
 
 
 def on_device(tokens, frozen_matrix, adapter_down_factor, adapter_up_factor, magnitude, cotangent):
@@ -382,7 +530,7 @@
 
 def solution(mesh):
     planes = mesh.shape["dp"] // PLANE
-    in_planes = mesh.shape["tensor"] == 1 and mesh.shape["dp"] == PLANE * planes and planes > 1
+    in_planes = mesh.shape["tensor"] == 1 and mesh.shape["dp"] == PLANE * planes and planes == 4
     return jax.shard_map(
         on_plane if in_planes else on_device,
         mesh=mesh,

time: 609 us -> 591 us (0.970)
  Pallas kernels: 286 us -> 384 us
  waiting for transfers between devices: 135 us -> 64.6 us
  between operations: 14.3 us -> 1.08 us
  matrix products: 94.1 us -> 83.9 us
  starting transfers between devices: 13.6 us -> 3.88 us
  other arithmetic: 21.7 us -> 13.6 us
    pallas_call x0 -> x1, Pallas kernels: none -> 175 us  [ring_exchange(): pl.pallas_call(functools.partial(ring_kernel, views, steps), out_shape=[j...]
    psum x1 -> x0, waiting for transfers between devices: 99.9 us -> none  [on_plane(): grad_down, grad_up = lax.psum((down_part, up_part), 'dp')]
    pallas_call x4 -> x3, Pallas kernels: 259 us -> 176 us  [exchange(): pl.pallas_call(functools.partial(exchange_kernel, views, vector), out_sha...]
    ppermute x14 -> x4, waiting for transfers between devices: 35.4 us -> 64.6 us  [the longest x1 33.2 us: on_plane(): falling = lax.ppermute(weights[steps][:, :2 * width], 'dp', forward)]
    dot_general x11 -> x12, matrix products: 87.6 us -> 75.6 us  [dot(): lax.dot_general(a, b, ((contract[:1], contract[1:]), ((), ())), preferred...]
    ppermute x14 -> x4, starting transfers between devices: 13.5 us -> 3.88 us  [the longest x1 3.31 us: on_plane(): lax.ppermute(weights[steps][:, 4 * width:6 * width], 'dp', backward)]
    pallas_call x5 -> x6, Pallas kernels: 27.7 us -> 33.6 us  [reorder(): pl.pallas_call(kernel, out_shape=jax.ShapeDtypeStruct((rows, outputs), ki...]
    unnamed x45 -> x65, local copies, waits for them, and re-layouts: 29 us -> 24.7 us
  transfers between devices with their start and end apart: 15 -> 4, of which waited for: 3 -> 2; matrix products, arithmetic and copies ran while one was open for 16% -> 4% of each run, Pallas kernels for 19% -> 1%
where the time goes in v3:
time: 591 us; the launch traced here: 589 us
  Pallas kernels  384 us (65%)
  matrix products  83.9 us (14%)
  waiting for transfers between devices  64.6 us (11%)
  local copies, waits for them, and re-layouts  37.8 us (6%)
  other arithmetic  13.6 us (2%)
    pallas_call x3, Pallas kernels, exchange(): pl.pallas_call(functools.partial(exchange_kernel, views, vector), out_sha...  176 us
    pallas_call x1, Pallas kernels, ring_exchange(): pl.pallas_call(functools.partial(ring_kernel, views, steps), out_shape=[j...  175 us
    dot_general x12, matrix products, dot(): lax.dot_general(a, b, ((contract[:1], contract[1:]), ((), ())), preferred...  75.6 us
    pallas_call x6, Pallas kernels, reorder(): pl.pallas_call(kernel, out_shape=jax.ShapeDtypeStruct((rows, outputs), ki...  33.6 us
    ppermute x1, waiting for transfers between devices, on_plane(): falling = lax.ppermute(weights[steps][:, :2 * width], 'dp', forward)  33.2 us
    ppermute x1, waiting for transfers between devices, on_plane(): lax.ppermute(weights[steps][:, 4 * width:6 * width], 'dp', backward)  31.3 us
    unnamed x65, local copies, waits for them, and re-layouts  24.7 us
  transfers between devices with their start and end apart: 4, of which 2 were waited for; matrix products, arithmetic and copies ran while one was open for 4% of the time, Pallas kernels for 1%

profile of v3, /device:TPU:0, one launch (start us, length us, event | category | flops | bytes accessed | tf_op | source)
XLA Modules:
  0.0 589.0 jit_solution(17625176734065559551)
XLA Ops:
  0.7 6.2 %copy.13 = bf16[14336,128]{0,1:T(8,128)(2,1)} copy(bf16[14336,128]{1,0:T(8,128)(2,1)} %refs_0_.1) | data formatting | bytes 7340032 | tf_op args[1]
  6.9 3.4 fusion.2
  10.8 48.8 %shard_map.101 = (bf16[2,3584,256]{2,1,0:T(8,128)(2,1)}, f32[8,4,8,128]{3,2,1,0:T(8,128)}) custom-call(bf16[14336,128]{1,0:T(8,128)(2,1)} %refs_0_.1, f32[8,128]{1,0:T(8,128)} %broadcast_in_dim.8.refs_1_), custom_call_target="tpu_custom_call" | custom-call | bytes 146800640 | tf_op jit(solution)/shard_map/pallas_call | solution.py:175
  63.4 5.9 %shard_map.102.refs_2_ = bf16[128,4096]{1,0:T(8,128)(2,1)} custom-call(s32[2]{0:T(128)} %pad_add_fusion.info, bf16[128,4096]{1,0:T(8,128)(2,1)} %x_ref.2), custom_call_target="tpu_custom_call" | custom-call | tf_op jit(solution)/shard_map/pallas_call | solution.py:314
  69.9 174.8 %shard_map.103 = (bf16[3584,1024]{1,0:T(8,128)(2,1)}, bf16[3584,1024]{1,0:T(8,128)(2,1)}, bf16[3584,1024]{1,0:T(8,128)(2,1)}, bf16[512,3584]{1,0:T(8,128)(2,1)},...) custom-call(bf16[2,3584,256]{2,1,0:T(8,128)(2,1)} %get-tuple-element.20.refs_0_, bf16[128,14336]{1,0:T(8,128)(2,1)} %refs_1_.1, ...), custom_call_target="tpu_custom_call" | custom-call | bytes 400000000 | tf_op jit(solution)/shard_map/pallas_call | solution.py:263
  251.1 7.7 %fusion.16 = f32[512,1024]{1,0:T(8,128)} fusion(bf16[512,3584]{1,0:T(8,128)(2,1)S(1)} %copy-done.7, bf16[3584,1024]{1,0:T(8,128)(2,1)} %get-tuple-element.24), kind=kOutput, calls=%fused_computation.46 | convolution fusion | flops 3758096384 | bytes 13107200 | tf_op jit(solution)/shard_map/dot_general | solution.py:367
  258.9 33.2 %collective-permute-done = bf16[3584,256]{1,0:T(8,128)(2,1)} collective-permute-done((bf16[3584,256]{1,0:T(8,128)(2,1)S(1)}, bf16[3584,256]{1,0:T(8,128)(2,1)}, u32[]{:S(2)}, u32[]{:S(2)}) %collective-permute-start) | collective-permute-done | bytes 1835040 | tf_op jit(solution)/shard_map/ppermute | solution.py:405
  292.2 5.3 fusion.15
  297.4 31.3 %collective-permute-done.2 = bf16[3584,256]{1,0:T(8,128)(2,1)} collective-permute-done((bf16[3584,256]{1,0:T(8,128)(2,1)S(1)}, bf16[3584,256]{1,0:T(8,128)(2,1)}, u32[]{:S(2)}, u32[]{:S(2)}) %collective-permute-start.2) | collective-permute-done | bytes 1835040 | tf_op jit(solution)/shard_map/ppermute | solution.py:406
  329.7 5.5 shard_map.107
  344.4 4.1 fusion.17
  350.3 8.2 %multiply_reduce_fusion.4 = (f32[1024]{0:T(1024)S(1)}, f32[1024]{0:T(1024)S(1)}, f32[1024]{0:T(1024)S(1)}, f32[1024]{0:T(1024)S(1)}, bf16[512,1024]{1,0:T(8,128)...) fusion(bf16[512,4096]{1,0:T(8,128)(2,1)} %get-tuple-element.25, ...), kind=kOutput, calls=%fused_computation.17 | convolution fusion | flops 3766480896 | bytes 25706496 | tf_op jit(solution)/shard_map/dot_general | solution.py:367
  359.2 4.8 shard_map.105
  366.2 4.8 shard_map.106
  375.0 10.8 %fusion.6 = f32[512,3584]{1,0:T(8,128)} fusion(bf16[3584,1024]{1,0:T(8,128)(2,1)} %get-tuple-element.22, bf16[512,4096]{1,0:T(8,128)(2,1)S(1)} %multiply_convert_fusion), kind=kOutput, calls=%fused_computation.25 | convolution fusion | flops 3758096384 | bytes 15728640 | tf_op jit(solution)/shard_map/dot_general | solution.py:367
  390.4 6.0 %shard_map.108 = f32[64,4096]{1,0:T(8,128)} custom-call(s32[2]{0:T(128)} %pad_add_fusion.info, f32[64,4096]{1,0:T(8,128)} %fusion.9.x_ref), custom_call_target="tpu_custom_call" | custom-call | tf_op jit(solution)/shard_map/pallas_call | solution.py:314
  396.3 7.3 %convolution_add_fusion = f32[512,3584]{1,0:T(8,128)} fusion(f32[512,3584]{1,0:T(8,128)} %fusion.6, bf16[512,64]{0,1:T(8,128)(2,1)S(1)} %convolution_convert_fusion, bf16[14336,64]{0,1:T(8,128)(2,1)S(1)} %copy-done, s32[]{:T(128)S(6)} %select_n.32), kind=kOutput, calls=%fused_computation.5 | convolution fusion | flops 236716032 | bytes 15204356 | tf_op jit(solution)/shard_map/dot_general | solution.py:367
  403.7 10.4 %convolution_add_fusion.2 = f32[512,3584]{1,0:T(8,128)} fusion(f32[512,3584]{1,0:T(8,128)} %convolution_add_fusion, bf16[3584,1024]{1,0:T(8,128)(2,1)} %get-tuple-element.23, bf16[512,4096]{1,0:T(8,128)(2,1)S(1)} %copy-done.3), kind=kOutput, calls=%fused_computation.8 | convolution fusion | flops 3759931392 | bytes 23068672 | tf_op jit(solution)/shard_map/dot_general | solution.py:367
  414.0 8.1 %convolution_add_fusion.1 = f32[512,3584]{1,0:T(8,128)} fusion(f32[512,3584]{1,0:T(8,128)} %convolution_add_fusion.2, bf16[3584,1024]{1,0:T(8,128)(2,1)S(1)} %bitcast.61, bf16[512,4096]{1,0:T(8,128)(2,1)S(1)} %copy-done.3), kind=kOutput, calls=%fused_computation.7 | convolution fusion | flops 3759931392 | bytes 23068672 | tf_op jit(solution)/shard_map/dot_general | solution.py:367
  422.2 9.8 %add_convert_fusion.refs_1_ = bf16[512,3584]{1,0:T(8,128)(2,1)} fusion(f32[512,3584]{1,0:T(8,128)} %convolution_add_fusion.1, bf16[3584,1024]{1,0:T(8,128)(2,1)} %copy-done.16, bf16[512,4096]{1,0:T(8,128)(2,1)S(1)} %copy-done.3), kind=kOutput, calls=%fused_computation.4 | convolution fusion | flops 3761766400 | bytes 19398656 | tf_op jit(solution)/shard_map/dot_general | solution.py:367
  433.8 38.1 %shard_map.104 = bf16[4,128,3072]{2,1,0:T(8,128)(2,1)} custom-call(bf16[512,3072]{1,0:T(8,128)(2,1)} %pad_maximum_fusion.refs_0_), custom_call_target="tpu_custom_call" | custom-call | bytes 125829120 | tf_op jit(solution)/shard_map/pallas_call | solution.py:175
  474.0 88.8 %shard_map.109 = (bf16[4,128,1024]{2,1,0:T(8,128)(2,1)}, bf16[128,14336]{1,0:T(8,128)(2,1)}, f32[32,128]{1,0:T(8,128)}, f32[2,4,4,8,4608]{4,3,2,1,0:T(8,128)}) custom-call(bf16[512,1024]{1,0:T(8,128)(2,1)} %get-tuple-element.28.refs_0_, bf16[512,3584]{1,0:T(8,128)(2,1)} %add_convert_fusion.refs_1_, f32[32,128]{1,0:T(8,128)} %bitcast.65, ...), custom_call_target="tpu_custom_call" | custom-call | bytes 188743680 | tf_op jit(solution)/shard_map/pallas_call | solution.py:175
  578.1 6.7 %shard_map.110 = bf16[128,4096]{1,0:T(8,128)(2,1)} custom-call(s32[2]{0:T(128)} %pad_add_fusion.info, f32[128,4096]{1,0:T(8,128)} %pad_maximum_fusion.1.x_ref, f32[128,4096]{1,0:T(8,128)} %get-tuple-element.49.adapter_ref, f32[1,4096]{1,0:T(1,128)} %bitcast.63), custom_call_target="tpu_custom_call" | custom-call | tf_op jit(solution)/shard_map/pallas_call | solution.py:314
  584.8 4.2 copy.27
  (103 shorter events, 53.8 us)
Async XLA Ops:
  0.6 6.2 %copy-start = (bf16[14336,64]{0,1:T(8,128)(2,1)S(1)}, bf16[14336,64]{0,1:T(8,128)(2,1)}, u32[]{:S(2)}) copy-start(bf16[14336,64]{0,1:T(8,128)(2,1)} %param.8) | copy-start | bytes 5505028
  244.8 6.4 %copy-start.7 = (bf16[512,3584]{1,0:T(8,128)(2,1)S(1)}, bf16[512,3584]{1,0:T(8,128)(2,1)}, u32[]{:S(2)}) copy-start(bf16[512,3584]{1,0:T(8,128)(2,1)} %get-tuple-element.21) | copy-start | bytes 11010052
  244.8 47.3 %slice-start.3 = ((s8[7340032]{0:T(1024)(128)(4,1)}), s8[4194304]{0:T(1024)(128)(4,1)S(1)}, s32[]{:S(2)}) async-start(s8[7340032]{0:T(1024)(128)(4,1)} %bitcast.68), calls=%async_computation.3 | async-start | bytes 8388608
  247.3 44.9 %collective-permute-start = (bf16[3584,256]{1,0:T(8,128)(2,1)S(1)}, bf16[3584,256]{1,0:T(8,128)(2,1)}, u32[]{:S(2)}, u32[]{:S(2)}) collective-permute-start(bf16[3584,256]{1,0:T(8,128)(2,1)S(1)} %get-tuple-element.40), channel_id=1, source_target_pairs={{0,8},{1,9},{2,10},{3,11},{4,12},{5,13},{6,14},{7,15},{8,16},{9,17... | collective-permute-start | bytes 5505032 | tf_op jit(solution)/shard_map/ppermute | solution.py:405
  247.8 80.9 %collective-permute-start.2 = (bf16[3584,256]{1,0:T(8,128)(2,1)S(1)}, bf16[3584,256]{1,0:T(8,128)(2,1)}, u32[]{:S(2)}, u32[]{:S(2)}) collective-permute-start(bf16[3584,256]{1,0:T(8,128)(2,1)S(1)} %get-tuple-element.39), channel_id=1, source_target_pairs={{8,0},{9,1},{10,2},{11,3},{12,4},{13,5},{14,6},{15,7},{16,8},{17,9... | collective-permute-start | bytes 5505032 | tf_op jit(solution)/shard_map/ppermute | solution.py:406
  251.1 41.0 %slice-start.4 = ((s8[7340032]{0:T(1024)(128)(4,1)}), s8[3145728]{0:T(1024)(128)(4,1)S(1)}, s32[]{:S(2)}) async-start(s8[7340032]{0:T(1024)(128)(4,1)} %bitcast.68), calls=%async_computation.4 | async-start | bytes 6291456
  292.1 46.6 %collective-permute-start.1 = (bf16[3584,256]{1,0:T(8,128)(2,1)}, bf16[3584,256]{1,0:T(8,128)(2,1)}, u32[]{:S(2)}, u32[]{:S(2)}) collective-permute-start(bf16[3584,256]{1,0:T(8,128)(2,1)} %collective-permute-done), channel_id=1, source_target_pairs={{0,1},{1,0},{2,3},{3,2},{4,5},{5,4},{6,7},{7,6},{8,9},{9,8},{10,11... | collective-permute-start | bytes 5505032 | tf_op jit(solution)/shard_map/ppermute | solution.py:408
  292.1 43.0 %copy-start.6 = (bf16[128,4096]{1,0:T(8,128)(2,1)S(1)}, bf16[128,4096]{1,0:T(8,128)(2,1)}, u32[]{:S(2)}) copy-start(bf16[128,4096]{1,0:T(8,128)(2,1)} %x_ref.2) | copy-start | bytes 3145732
  292.1 43.0 %copy-start.10 = (bf16[64,4096]{1,0:T(8,128)(2,1)S(1)}, bf16[64,4096]{1,0:T(8,128)(2,1)}, u32[]{:S(2)}) copy-start(bf16[64,4096]{1,0:T(8,128)(2,1)} %x_ref.3) | copy-start | bytes 1572868
  328.7 13.7 %collective-permute-start.3 = (bf16[3584,256]{1,0:T(8,128)(2,1)}, bf16[3584,256]{1,0:T(8,128)(2,1)}, u32[]{:S(2)}, u32[]{:S(2)}) collective-permute-start(bf16[3584,256]{1,0:T(8,128)(2,1)} %collective-permute-done.2), channel_id=1, source_target_pairs={{0,1},{1,0},{2,3},{3,2},{4,5},{5,4},{6,7},{7,6},{8,9},{9,8},{10,11... | collective-permute-start | bytes 5505032 | tf_op jit(solution)/shard_map/ppermute | solution.py:408
  342.4 6.1 %slice-start.5 = ((s8[7340032]{0:T(1024)(128)(4,1)}), s8[4194304]{0:T(1024)(128)(4,1)S(1)}, s32[]{:S(2)}) async-start(s8[7340032]{0:T(1024)(128)(4,1)} %bitcast.70), calls=%async_computation.5 | async-start | bytes 8388608
  344.4 5.4 copy-start.21
  344.4 5.9 %copy-start.22 = (f32[512,1024]{1,0:T(8,128)S(1)}, f32[512,1024]{1,0:T(8,128)}, u32[]{:S(2)}) copy-start(f32[512,1024]{1,0:T(8,128)} %fusion.15) | copy-start | bytes 6291460
  350.3 14.6 %copy-start.20 = (bf16[4096]{0:T(1024)(128)(2,1)S(1)}, bf16[4096]{0:T(1024)(128)(2,1)}, u32[]{:S(2)}) copy-start(bf16[4096]{0:T(1024)(128)(2,1)} %param.10) | copy-start | bytes 24580
  365.5 9.4 %copy-start.17 = (f32[4096]{0:T(1024)}, f32[4096]{0:T(1024)S(1)}, u32[]{:S(2)}) copy-start(f32[4096]{0:T(1024)S(1)} %get-tuple-element.45) | copy-start | bytes 49156
  375.0 13.6 %copy-start.2 = (bf16[512,4096]{1,0:T(8,128)(2,1)}, bf16[512,4096]{1,0:T(8,128)(2,1)S(1)}, u32[]{:S(2)}) copy-start(bf16[512,4096]{1,0:T(8,128)(2,1)S(1)} %multiply_convert_fusion) | copy-start | bytes 12582916
  375.0 10.8 %copy-start.11 = (bf16[64,4096]{1,0:T(8,128)(2,1)S(1)}, bf16[64,4096]{1,0:T(8,128)(2,1)}, u32[]{:S(2)}) copy-start(bf16[64,4096]{1,0:T(8,128)(2,1)} %shard_map.107) | copy-start | bytes 1572868
  396.3 7.3 %copy-start.3 = (bf16[512,4096]{1,0:T(8,128)(2,1)S(1)}, bf16[512,4096]{1,0:T(8,128)(2,1)}, u32[]{:S(2)}) copy-start(bf16[512,4096]{1,0:T(8,128)(2,1)} %copy-done.2) | copy-start | bytes 12582916
  396.3 17.7 %slice-start.1 = ((s8[7340032]{0:T(1024)(128)(4,1)}), s8[4194304]{0:T(1024)(128)(4,1)S(1)}, s32[]{:S(2)}) async-start(s8[7340032]{0:T(1024)(128)(4,1)} %bitcast.60), calls=%async_computation.1 | async-start | bytes 8388608
  403.7 10.4 %slice-start.2 = ((s8[7340032]{0:T(1024)(128)(4,1)}), s8[3145728]{0:T(1024)(128)(4,1)S(1)}, s32[]{:S(2)}) async-start(s8[7340032]{0:T(1024)(128)(4,1)} %bitcast.60), calls=%async_computation.2 | async-start | bytes 6291456
  422.2 9.8 %copy-start.13 = (bf16[512,1024]{1,0:T(8,128)(2,1)S(1)}, bf16[512,1024]{1,0:T(8,128)(2,1)}, u32[]{:S(2)}) copy-start(bf16[512,1024]{1,0:T(8,128)(2,1)} %get-tuple-element.41) | copy-start | bytes 3145732
  422.2 9.8 %copy-start.14 = (bf16[512,1024]{1,0:T(8,128)(2,1)S(1)}, bf16[512,1024]{1,0:T(8,128)(2,1)}, u32[]{:S(2)}) copy-start(bf16[512,1024]{1,0:T(8,128)(2,1)} %get-tuple-element.42) | copy-start | bytes 3145732
  422.2 9.8 %copy-start.15 = (bf16[512,1024]{1,0:T(8,128)(2,1)S(1)}, bf16[512,1024]{1,0:T(8,128)(2,1)}, u32[]{:S(2)}) copy-start(bf16[512,1024]{1,0:T(8,128)(2,1)} %get-tuple-element.44) | copy-start | bytes 3145732
  578.1 10.9 %copy-start.1 = (bf16[14336,64]{0,1:T(8,128)(2,1)S(1)}, bf16[14336,64]{0,1:T(8,128)(2,1)}, u32[]{:S(2)}) copy-start(bf16[14336,64]{0,1:T(8,128)(2,1)} %param.8) | copy-start | bytes 5505028
  (10 other events, 32.3 us)

commit v4 on v3

--- a/solution.py
+++ b/solution.py
@@ -271,7 +271,7 @@
         compiler_params=pltpu.CompilerParams(
             collective_id=collective_id, has_side_effects=True
         ),
-        cost_estimate=pl.CostEstimate(flops=0, bytes_accessed=400_000_000, transcendentals=0),
+        cost_estimate=pl.CostEstimate(flops=0, bytes_accessed=350_000_000, transcendentals=0),
     )(blocks, *sources)
 
 
@@ -389,7 +389,7 @@
         [jax.ShapeDtypeStruct((2, depth, 2 * width), bf16)], 1, "gather", squares,
     )
     rank_act = jnp.dot(tokens, down, preferred_element_type=f32).astype(bf16)
-    steps = planes - 2
+    steps = 1
     *weights, tokens_part, cotangent_part, rank_part = ring_exchange(
         blocks, steps, [rows_to_columns(depth), whole_rows, whole_rows],
         [tokens, reorder(to_arrival, [cotangent], bf16, True, info, planes),
@@ -402,12 +402,15 @@
     forward = [(i, (i + PLANE) % size) for i in range(size)]
     backward = [((i + PLANE) % size, i) for i in range(size)]
     across = [(i, i - i % CORES + (i + 1) % CORES) for i in range(size)]
-    falling = lax.ppermute(weights[steps][:, : 2 * width], "dp", forward)
-    rising = lax.ppermute(weights[steps][:, 4 * width : 6 * width], "dp", backward)
-    last = jnp.concatenate(
-        [falling, lax.ppermute(falling, "dp", across), rising, lax.ppermute(rising, "dp", across)],
-        axis=1,
-    )
+
+    def pass_on(pair):
+        return lax.ppermute(pair[0], "dp", forward), lax.ppermute(pair[1], "dp", backward)
+
+    def with_other(pair):
+        falling, rising = (lax.ppermute(part, "dp", across) for part in pair)
+        return jnp.concatenate([pair[0], falling, pair[1], rising], axis=1)
+
+    arriving = pass_on((weights[steps][:, : 2 * width], weights[steps][:, 4 * width : 6 * width]))
 
     norm = jnp.sqrt(squares[:, :, 0, :].transpose(1, 0, 2).reshape(outputs) + epsilon)
     scale = magnitude.astype(f32) / norm
@@ -433,29 +436,42 @@
     terms = terms.reshape(CORES, planes, rank // (CORES * planes), terms.shape[1])
 
     partial, sums = [], []
-    for step in range(planes):
-        weight = weights[step] if step <= steps else last
+
+    def apply(step, weight, gradient):
         columns = slice(step * block, (step + 1) * block)
         out = dot(tokens_part, weight, (1, 0))
         gradient = gradient + dot(grad_part[:, columns], weight, (1, 1))
-        if step < planes - 1:
-            gradient = lax.optimization_barrier(gradient)
         sums.append(jnp.sum(cotangent_part[:, columns].astype(f32) * out, axis=0))
         partial.append(out.astype(bf16))
-
-    early = jnp.concatenate(partial[:-1], axis=1)
-    late = partial[-1]
-    (early_slots,) = exchange(
-        [rows_to_slots(rows)], [early],
-        [jax.ShapeDtypeStruct((CHIPS, rows, early.shape[1]), bf16)], 3,
-    )
+        return gradient
+
+    for step in range(steps + 1):
+        gradient = lax.optimization_barrier(apply(step, weights[step], gradient))
+    early = jnp.concatenate(partial, axis=1)
+    arriving, gradient, early, sums, terms = lax.optimization_barrier(
+        (arriving, gradient, early, sums, terms)
+    )
+    for step in range(steps + 1, planes):
+        pair = arriving
+        if step < planes - 1:
+            arriving = pass_on(pair)
+        gradient = apply(step, with_other(pair), gradient)
+        if step == steps + 1:
+            (early_slots,) = exchange(
+                [rows_to_slots(rows)], [early],
+                [jax.ShapeDtypeStruct((CHIPS, rows, early.shape[1]), bf16)], 3,
+            )
+        if step < planes - 1:
+            arriving, gradient, early_slots, partial, sums = lax.optimization_barrier(
+                (arriving, gradient, early_slots, partial, sums)
+            )
+    late = jnp.concatenate(partial[steps + 1 :], axis=1)
     sums = jnp.broadcast_to(jnp.concatenate(sums)[None], (8, outputs))
     sums = reorder(from_arrival, [sums], f32, False, info, planes)[0]
     sums = (sums + jnp.sum(cot_own * adapter, axis=0)) / norm
-    early_slots, late, sums = lax.optimization_barrier((early_slots, late, sums))
     late_slots, input_gradient, grad_magnitude, totals = exchange(
         [rows_to_slots(rows), columns_to_rows(rows, depth)], [late, gradient.astype(bf16)],
-        [jax.ShapeDtypeStruct((CHIPS, rows, block), bf16),
+        [jax.ShapeDtypeStruct((CHIPS, rows, late.shape[1]), bf16),
          jax.ShapeDtypeStruct((rows, features), bf16)], 4,
         "sum", sums.reshape(outputs // 128, 128), terms,
     )

time: 591 us -> 582 us (0.985)
  waiting for transfers between devices: 64.6 us -> 24.5 us
  other arithmetic: 13.6 us -> 34 us
    ppermute x4 -> x8, waiting for transfers between devices: 64.6 us -> 24.5 us  [the longest x2 24.4 us: pass_on(): lax.ppermute(pair[1], 'dp', backward)]
    add x0 -> x1, other arithmetic: none -> 9.67 us  [apply(): gradient = gradient + dot(grad_part[:, columns], weight, (1, 1))]
    convert_element_type x0 -> x1, other arithmetic: none -> 8.14 us  [on_plane(): gradient.astype(bf16)]
    unnamed x65 -> x60, local copies, waits for them, and re-layouts: 24.7 us -> 29.5 us
  transfers between devices with their start and end apart: 4 -> 8, of which waited for: 2 -> 2; matrix products, arithmetic and copies ran while one was open for 4% -> 16% of each run, Pallas kernels for 1% -> 7%
where the time goes in v4:
time: 582 us; the launch traced here: 575 us
  Pallas kernels  382 us (66%)
  matrix products  80.4 us (14%)
  local copies, waits for them, and re-layouts  43 us (7%)
  other arithmetic  34 us (6%)
  waiting for transfers between devices  24.5 us (4%)
  starting transfers between devices  8.82 us (2%)
    pallas_call x1, Pallas kernels, ring_exchange(): pl.pallas_call(functools.partial(ring_kernel, views, steps), out_shape=[j...  175 us
    pallas_call x3, Pallas kernels, exchange(): pl.pallas_call(functools.partial(exchange_kernel, views, vector), out_sha...  174 us
    dot_general x12, matrix products, dot(): lax.dot_general(a, b, ((contract[:1], contract[1:]), ((), ())), preferred...  72.2 us
    pallas_call x6, Pallas kernels, reorder(): pl.pallas_call(kernel, out_shape=jax.ShapeDtypeStruct((rows, outputs), ki...  33.8 us
    unnamed x60, local copies, waits for them, and re-layouts  29.5 us
    ppermute x2, waiting for transfers between devices, pass_on(): lax.ppermute(pair[1], 'dp', backward)  24.4 us
  transfers between devices with their start and end apart: 8, of which 2 were waited for; matrix products, arithmetic and copies ran while one was open for 16% of the time, Pallas kernels for 7%

profile of v4, /device:TPU:0, one launch (start us, length us, event | category | flops | bytes accessed | tf_op | source)
XLA Modules:
  0.0 574.5 jit_solution(14138495237686757854)
XLA Ops:
  0.7 6.2 %copy.14 = bf16[14336,128]{0,1:T(8,128)(2,1)} copy(bf16[14336,128]{1,0:T(8,128)(2,1)} %refs_0_.1) | data formatting | bytes 7340032 | tf_op args[1]
  10.9 48.8 %shard_map.101 = (bf16[2,3584,256]{2,1,0:T(8,128)(2,1)}, f32[8,4,8,128]{3,2,1,0:T(8,128)}) custom-call(bf16[14336,128]{1,0:T(8,128)(2,1)} %refs_0_.1, f32[8,128]{1,0:T(8,128)} %broadcast_in_dim.8.refs_1_), custom_call_target="tpu_custom_call" | custom-call | bytes 146800640 | tf_op jit(solution)/shard_map/pallas_call | solution.py:175
  63.4 5.9 %shard_map.102.refs_2_ = bf16[128,4096]{1,0:T(8,128)(2,1)} custom-call(s32[2]{0:T(128)} %pad_add_fusion.info, bf16[128,4096]{1,0:T(8,128)(2,1)} %x_ref.2), custom_call_target="tpu_custom_call" | custom-call | tf_op jit(solution)/shard_map/pallas_call | solution.py:314
  69.9 174.7 %shard_map.103 = (bf16[3584,1024]{1,0:T(8,128)(2,1)}, bf16[3584,1024]{1,0:T(8,128)(2,1)}, bf16[512,3584]{1,0:T(8,128)(2,1)}, bf16[512,4096]{1,0:T(8,128)(2,1)}, bf16[512,128]{1,0:T(8,128)(2,1)}) custom-call(bf16[2,3584,256]{2,1,0:T(8,128)(2,1)} %get-tuple-element.31.refs_0_, bf16[128,14336]{1,0:T(8,128)(2,1)} %refs_1_.1, ...), custom_call_target="tpu_custom_call" | custom-call | bytes 350000000 | tf_op jit(solution)/shard_map/pallas_call | solution.py:263
  252.8 5.5 shard_map.105
  259.9 4.8 shard_map.104
  270.2 10.5 %fusion.8 = f32[512,3584]{1,0:T(8,128)} fusion(bf16[3584,1024]{1,0:T(8,128)(2,1)} %get-tuple-element.35, bf16[512,4096]{1,0:T(8,128)(2,1)S(1)} %multiply_convert_fusion), kind=kOutput, calls=%fused_computation.27 | convolution fusion | flops 3758096384 | bytes 15728640 | tf_op jit(solution)/shard_map/dot_general | solution.py:367
  280.7 5.3 fusion.17
  286.0 4.2 convolution_add_fusion
  290.2 10.7 %convolution_add_fusion.1 = f32[512,3584]{1,0:T(8,128)} fusion(f32[512,3584]{1,0:T(8,128)S(1)} %convolution_add_fusion, bf16[3584,1024]{1,0:T(8,128)(2,1)} %get-tuple-element.32, bf16[512,4096]{1,0:T(8,128)(2,1)} %copy-done.2), kind=kOutput, calls=%fused_computation.6 | convolution fusion | flops 3759931392 | bytes 23068672 | tf_op jit(solution)/shard_map/dot_general | solution.py:367
  300.9 9.1 %multiply_reduce_fusion.3 = (f32[1024]{0:T(1024)S(1)}, f32[1024]{0:T(1024)S(1)}, bf16[512,1024]{1,0:T(8,128)(2,1)S(1)}, bf16[512,1024]{1,0:T(8,128)(2,1)}) fusion(bf16[512,4096]{1,0:T(8,128)(2,1)} %get-tuple-element.33, f32[512,1024]{1,0:T(8,128)S(1)} %copy-done.22, bf16[512,3584]{1,0:T(8,128)(2,1)S(1)} %copy-done.9, bf16[3584,1024]{1,0:T(8,128)(2,1)} %get-tuple-element.32), kind=kOutput, calls=%fused_computation.16 | convolution fusion | flops 3762288640 | bytes 17309696 | tf_op jit(solution)/shard_map/dot_general | solution.py:367
  314.0 5.9 %shard_map.106 = f32[64,4096]{1,0:T(8,128)} custom-call(s32[2]{0:T(128)} %pad_add_fusion.info, f32[64,4096]{1,0:T(8,128)} %fusion.11.x_ref), custom_call_target="tpu_custom_call" | custom-call | tf_op jit(solution)/shard_map/pallas_call | solution.py:314
  325.7 4.9 collective-permute-done.1
  334.9 25.6 %shard_map.107 = bf16[4,128,2048]{2,1,0:T(8,128)(2,1)} custom-call(bf16[512,2048]{1,0:T(8,128)(2,1)} %pad_maximum_fusion.refs_0_), custom_call_target="tpu_custom_call" | custom-call | bytes 83886080 | tf_op jit(solution)/shard_map/pallas_call | solution.py:175
  369.2 6.1 %fusion.5 = f32[512,3584]{1,0:T(8,128)} fusion(bf16[3584,1024]{1,0:T(8,128)(2,1)S(1)} %constant_dynamic-update-slice_fusion, bf16[512,4096]{1,0:T(8,128)(2,1)S(1)} %copy-done.3), kind=kOutput, calls=%fused_computation.24 | convolution fusion | flops 3758096384 | bytes 15728640 | tf_op jit(solution)/shard_map/dot_general | solution.py:367
  375.3 9.7 %add.62 = f32[512,3584]{1,0:T(8,128)} add(f32[512,3584]{1,0:T(8,128)} %convolution_add_fusion.1, f32[512,3584]{1,0:T(8,128)} %fusion.5) | non-fusion elementwise | flops 1835008 | bytes 22020096 | tf_op jit(solution)/shard_map/add | solution.py:443
  384.9 9.2 %multiply_reduce_fusion.2 = (f32[1024]{0:T(1024)S(1)}, bf16[512,1024]{1,0:T(8,128)(2,1)}) fusion(bf16[512,4096]{1,0:T(8,128)(2,1)S(1)} %copy-done.7, bf16[512,3584]{1,0:T(8,128)(2,1)} %get-tuple-element.36, bf16[3584,1024]{1,0:T(8,128)(2,1)} %copy-done.17), kind=kOutput, calls=%fused_computation.15 | convolution fusion | flops 3760192512 | bytes 13111296 | tf_op jit(solution)/shard_map/dot_general | solution.py:367
  394.2 19.5 %collective-permute-done.3 = bf16[3584,256]{1,0:T(8,128)(2,1)} collective-permute-done((bf16[3584,256]{1,0:T(8,128)(2,1)}, bf16[3584,256]{1,0:T(8,128)(2,1)}, u32[]{:S(2)}, u32[]{:S(2)}) %collective-permute-start.3) | collective-permute-done | bytes 1835040 | tf_op jit(solution)/shard_map/ppermute | solution.py:407
  421.0 4.9 multiply_reduce_fusion.1
  425.9 6.1 %fusion.3 = f32[512,3584]{1,0:T(8,128)} fusion(bf16[3584,1024]{1,0:T(8,128)(2,1)S(1)} %constant_dynamic-update-slice_fusion.4, bf16[512,4096]{1,0:T(8,128)(2,1)S(1)} %copy-done.3), kind=kOutput, calls=%fused_computation.22 | convolution fusion | flops 3758096384 | bytes 15728640 | tf_op jit(solution)/shard_map/dot_general | solution.py:367
  432.7 5.0 shard_map.108
  439.2 8.1 %add_convert_fusion.refs_1_ = bf16[512,3584]{1,0:T(8,128)(2,1)} fusion(f32[512,3584]{1,0:T(8,128)} %add.62, f32[512,3584]{1,0:T(8,128)} %fusion.3), kind=kLoop, calls=%fused_computation.4 | loop fusion | flops 3670016 | bytes 18350080 | tf_op jit(solution)/shard_map/convert_element_type | solution.py:473
  448.9 99.4 %shard_map.109 = (bf16[4,128,2048]{2,1,0:T(8,128)(2,1)}, bf16[128,14336]{1,0:T(8,128)(2,1)}, f32[32,128]{1,0:T(8,128)}, f32[2,4,4,8,4608]{4,3,2,1,0:T(8,128)}) custom-call(bf16[512,2048]{1,0:T(8,128)(2,1)} %pad_maximum_fusion.1.refs_0_, bf16[512,3584]{1,0:T(8,128)(2,1)} %add_convert_fusion.refs_1_, f32[32,128]{1,0:T(8,128)} %bitcast_multiply_fusion.refs_2_, ...), custom_call_target="tpu_custom_call" | custom-call | bytes 230686720 | tf_op jit(solution)/shard_map/pallas_call | solution.py:175
  563.2 6.7 %shard_map.110 = bf16[128,4096]{1,0:T(8,128)(2,1)} custom-call(s32[2]{0:T(128)} %pad_add_fusion.info, f32[128,4096]{1,0:T(8,128)} %pad_maximum_fusion.2.x_ref, f32[128,4096]{1,0:T(8,128)} %get-tuple-element.71.adapter_ref, f32[1,4096]{1,0:T(1,128)} %bitcast.65), custom_call_target="tpu_custom_call" | custom-call | tf_op jit(solution)/shard_map/pallas_call | solution.py:314
  (109 shorter events, 76.2 us)
Async XLA Ops:
  244.7 14.5 %copy-start.21 = (bf16[4096]{0:T(1024)(128)(2,1)S(1)}, bf16[4096]{0:T(1024)(128)(2,1)}, u32[]{:S(2)}) copy-start(bf16[4096]{0:T(1024)(128)(2,1)} %param.10) | copy-start | bytes 24580
  248.8 76.9 %collective-permute-start = (bf16[3584,256]{1,0:T(8,128)(2,1)}, bf16[3584,256]{1,0:T(8,128)(2,1)}, u32[]{:S(2)}, u32[]{:S(2)}) collective-permute-start(bf16[3584,256]{1,0:T(8,128)(2,1)} %get-tuple-element.60), channel_id=1, source_target_pairs={{0,8},{1,9},{2,10},{3,11},{4,12},{5,13},{6,14},{7,15},{8,16},{9,17... | collective-permute-start | bytes 5505032 | tf_op jit(solution)/shard_map/ppermute | solution.py:407
  249.3 81.3 %collective-permute-start.1 = (bf16[3584,256]{1,0:T(8,128)(2,1)}, bf16[3584,256]{1,0:T(8,128)(2,1)}, u32[]{:S(2)}, u32[]{:S(2)}) collective-permute-start(bf16[3584,256]{1,0:T(8,128)(2,1)} %get-tuple-element.59), channel_id=1, source_target_pairs={{8,0},{9,1},{10,2},{11,3},{12,4},{13,5},{14,6},{15,7},{16,8},{17,9... | collective-permute-start | bytes 5505032 | tf_op jit(solution)/shard_map/ppermute | solution.py:407
  259.2 9.6 %copy-start.18 = (f32[4096]{0:T(1024)}, f32[4096]{0:T(1024)S(1)}, u32[]{:S(2)}) copy-start(f32[4096]{0:T(1024)S(1)} %bitcast_multiply_fusion.1) | copy-start | bytes 49156
  268.8 11.9 %copy-start.2 = (bf16[512,4096]{1,0:T(8,128)(2,1)}, bf16[512,4096]{1,0:T(8,128)(2,1)S(1)}, u32[]{:S(2)}) copy-start(bf16[512,4096]{1,0:T(8,128)(2,1)S(1)} %multiply_convert_fusion) | copy-start | bytes 12582916
  268.8 11.9 %slice-start.1 = ((s8[7340032]{0:T(1024)(128)(4,1)}), s8[4194304]{0:T(1024)(128)(4,1)S(1)}, s32[]{:S(2)}) async-start(s8[7340032]{0:T(1024)(128)(4,1)} %bitcast.70), calls=%async_computation.1 | async-start | bytes 8388608
  270.2 10.5 %copy-start.8 = (bf16[512,3584]{1,0:T(8,128)(2,1)S(1)}, bf16[512,3584]{1,0:T(8,128)(2,1)}, u32[]{:S(2)}) copy-start(bf16[512,3584]{1,0:T(8,128)(2,1)} %get-tuple-element.36) | copy-start | bytes 11010052
  270.2 10.5 %slice-start.2 = ((s8[7340032]{0:T(1024)(128)(4,1)}), s8[3145728]{0:T(1024)(128)(4,1)S(1)}, s32[]{:S(2)}) async-start(s8[7340032]{0:T(1024)(128)(4,1)} %bitcast.70), calls=%async_computation.2 | async-start | bytes 6291456
  290.2 10.7 %copy-start.9 = (bf16[512,3584]{1,0:T(8,128)(2,1)S(1)}, bf16[512,3584]{1,0:T(8,128)(2,1)}, u32[]{:S(2)}) copy-start(bf16[512,3584]{1,0:T(8,128)(2,1)} %get-tuple-element.36) | copy-start | bytes 11010052
  290.2 10.7 %copy-start.22 = (f32[512,1024]{1,0:T(8,128)S(1)}, f32[512,1024]{1,0:T(8,128)}, u32[]{:S(2)}) copy-start(f32[512,1024]{1,0:T(8,128)} %fusion.17) | copy-start | bytes 6291460
  300.9 9.1 %copy-start.19 = (bf16[512,128]{1,0:T(8,128)(2,1)S(1)}, bf16[512,128]{1,0:T(8,128)(2,1)}, u32[]{:S(2)}) copy-start(bf16[512,128]{1,0:T(8,128)(2,1)} %get-tuple-element.37) | copy-start | bytes 393220
  330.6 31.7 %collective-permute-start.4 = (bf16[3584,256]{1,0:T(8,128)(2,1)}, bf16[3584,256]{1,0:T(8,128)(2,1)}, u32[]{:S(2)}, u32[]{:S(2)}) collective-permute-start(bf16[3584,256]{1,0:T(8,128)(2,1)} %collective-permute-done), channel_id=1, source_target_pairs={{0,1},{1,0},{2,3},{3,2},{4,5},{5,4},{6,7},{7,6},{8,9},{9,8},{10,11... | collective-permute-start | bytes 5505032 | tf_op jit(solution)/shard_map/ppermute | solution.py:410
  330.6 35.4 %collective-permute-start.5 = (bf16[3584,256]{1,0:T(8,128)(2,1)}, bf16[3584,256]{1,0:T(8,128)(2,1)S(1)}, u32[]{:S(2)}, u32[]{:S(2)}) collective-permute-start(bf16[3584,256]{1,0:T(8,128)(2,1)} %collective-permute-done.1), channel_id=1, source_target_pairs={{0,1},{1,0},{2,3},{3,2},{4,5},{5,4},{6,7},{7,6},{8,9},{9,8},{10,11... | collective-permute-start | bytes 5505032 | tf_op jit(solution)/shard_map/ppermute | solution.py:410
  331.1 63.1 %collective-permute-start.2 = (bf16[3584,256]{1,0:T(8,128)(2,1)}, bf16[3584,256]{1,0:T(8,128)(2,1)}, u32[]{:S(2)}, u32[]{:S(2)}) collective-permute-start(bf16[3584,256]{1,0:T(8,128)(2,1)} %collective-permute-done), channel_id=1, source_target_pairs={{0,8},{1,9},{2,10},{3,11},{4,12},{5,13},{6,14},{7,15},{8,16},{9,17... | collective-permute-start | bytes 5505032 | tf_op jit(solution)/shard_map/ppermute | solution.py:407
  332.4 81.3 %collective-permute-start.3 = (bf16[3584,256]{1,0:T(8,128)(2,1)}, bf16[3584,256]{1,0:T(8,128)(2,1)}, u32[]{:S(2)}, u32[]{:S(2)}) collective-permute-start(bf16[3584,256]{1,0:T(8,128)(2,1)} %collective-permute-done.1), channel_id=1, source_target_pairs={{8,0},{9,1},{10,2},{11,3},{12,4},{13,5},{14,6},{15,7},{16,8},{17,9... | collective-permute-start | bytes 5505032 | tf_op jit(solution)/shard_map/ppermute | solution.py:407
  375.3 9.7 %copy-start.7 = (bf16[512,4096]{1,0:T(8,128)(2,1)S(1)}, bf16[512,4096]{1,0:T(8,128)(2,1)}, u32[]{:S(2)}) copy-start(bf16[512,4096]{1,0:T(8,128)(2,1)} %get-tuple-element.33) | copy-start | bytes 12582916
  384.9 29.3 %copy-start.6 = (bf16[128,4096]{1,0:T(8,128)(2,1)S(1)}, bf16[128,4096]{1,0:T(8,128)(2,1)}, u32[]{:S(2)}) copy-start(bf16[128,4096]{1,0:T(8,128)(2,1)} %x_ref.2) | copy-start | bytes 3145732
  384.9 29.3 %copy-start.13 = (bf16[64,4096]{1,0:T(8,128)(2,1)S(1)}, bf16[64,4096]{1,0:T(8,128)(2,1)}, u32[]{:S(2)}) copy-start(bf16[64,4096]{1,0:T(8,128)(2,1)} %x_ref.3) | copy-start | bytes 1572868
  394.2 21.8 %copy-start.5 = (bf16[4,128,2048]{2,1,0:T(8,128)(2,1)S(1)}, bf16[4,128,2048]{2,1,0:T(8,128)(2,1)}, u32[]{:S(2)}) copy-start(bf16[4,128,2048]{2,1,0:T(8,128)(2,1)} %shard_map.107) | copy-start | bytes 6291460
  413.7 4.4 collective-permute-start.6
  413.7 6.6 %collective-permute-start.7 = (bf16[3584,256]{1,0:T(8,128)(2,1)}, bf16[3584,256]{1,0:T(8,128)(2,1)S(1)}, u32[]{:S(2)}, u32[]{:S(2)}) collective-permute-start(bf16[3584,256]{1,0:T(8,128)(2,1)} %collective-permute-done.3), channel_id=1, source_target_pairs={{0,1},{1,0},{2,3},{3,2},{4,5},{5,4},{6,7},{7,6},{8,9},{9,8},{10,11... | collective-permute-start | bytes 5505032 | tf_op jit(solution)/shard_map/ppermute | solution.py:410
  439.2 8.1 %copy-start.15 = (bf16[512,1024]{1,0:T(8,128)(2,1)S(1)}, bf16[512,1024]{1,0:T(8,128)(2,1)}, u32[]{:S(2)}) copy-start(bf16[512,1024]{1,0:T(8,128)(2,1)} %get-tuple-element.45) | copy-start | bytes 3145732
  439.2 8.1 %copy-start.16 = (bf16[512,1024]{1,0:T(8,128)(2,1)S(1)}, bf16[512,1024]{1,0:T(8,128)(2,1)}, u32[]{:S(2)}) copy-start(bf16[512,1024]{1,0:T(8,128)(2,1)} %get-tuple-element.62) | copy-start | bytes 3145732
  563.2 10.9 %copy-start.1 = (bf16[14336,64]{0,1:T(8,128)(2,1)S(1)}, bf16[14336,64]{0,1:T(8,128)(2,1)}, u32[]{:S(2)}) copy-start(bf16[14336,64]{0,1:T(8,128)(2,1)} %param.8) | copy-start | bytes 5505028
  (10 other events, 37.0 us)

commit v5 on v4

--- a/solution.py
+++ b/solution.py
@@ -185,96 +185,6 @@
     )(*sources)
 
 
-def ring_kernel(views, steps, *refs):
-    count = len(views)
-    blocks, sources = refs[0], refs[1 : 1 + count]
-    weights, refs = refs[1 + count : 2 + count + steps], refs[2 + count + steps :]
-    targets = refs[:count]
-    send_sem, recv_sem, ring_send, ring_recv, side_send, side_recv, local_sem = refs[count:]
-    me = lax.axis_index("dp")
-    size = lax.axis_size("dp")
-    plane, chip, core = place()
-    base = me - chip * CORES
-    sibling = me - core + (core + 1) % CORES
-    after, before = (me + PLANE) % size, (me + size - PLANE) % size
-    width = blocks.shape[2]
-
-    def remote(source, target, send, recv, device):
-        return pltpu.make_async_remote_copy(
-            src_ref=source, dst_ref=target, send_sem=send, recv_sem=recv,
-            device_id={"dp": device}, device_id_type=pl.DeviceIdType.MESH,
-        )
-
-    partners = [base + ((chip + hop) % CHIPS) * CORES for hop in range(1, CHIPS)]
-    partners += [sibling, after, before]
-    barrier = pltpu.get_barrier_semaphore()
-    for device in partners:
-        pl.semaphore_signal(
-            barrier, inc=1, device_id={"dp": device}, device_id_type=pl.DeviceIdType.MESH
-        )
-    pl.semaphore_wait(barrier, len(partners))
-
-    def spot(step, side, other):
-        return weights[step].at[:, pl.ds((side * 2 + other) * width, width)]
-
-    def send(step):
-        ring, across = [], []
-        for side, device in enumerate((after, before)):
-            source = blocks.at[side] if step == 0 else spot(step, side, 0)
-            if step < steps:
-                ring.append(remote(source, spot(step + 1, side, 0), ring_send.at[step, side],
-                                   ring_recv.at[step, side], device))
-                ring[-1].start()
-            across.append(remote(source, spot(step, side, 1), side_send.at[step, side],
-                                 side_recv.at[step, side], sibling))
-            across[-1].start()
-        return ring, across
-
-    ring, copies = send(0)
-    for number, view in enumerate(views):
-        for hop in (2, 1, 3):
-            other = (chip + hop) % CHIPS
-            source, target = view(sources[number], targets[number], other, chip)
-            copies.append(remote(source, target, send_sem.at[number, hop],
-                                 recv_sem.at[number, hop], base + other * CORES))
-            copies[-1].start()
-    for number, view in enumerate(views):
-        source, target = view(sources[number], targets[number], chip, chip)
-        copies.append(pltpu.make_async_copy(source, target, local_sem.at[number]))
-        copies[-1].start()
-    for side in range(2):
-        copies.append(pltpu.make_async_copy(
-            blocks.at[side], spot(0, side, 0), local_sem.at[count + side]))
-        copies[-1].start()
-    for step in range(1, steps + 1):
-        for copy in ring:
-            copy.wait()
-        ring, across = send(step)
-        copies += across
-    for copy in copies:
-        copy.wait()
-
-
-def ring_exchange(blocks, steps, views, sources, shapes, collective_id):
-    count = len(views)
-    _, depth, width = blocks.shape
-    dma = pltpu.SemaphoreType.DMA
-    anywhere = pl.BlockSpec(memory_space=pl.ANY)
-    return pl.pallas_call(
-        functools.partial(ring_kernel, views, steps),
-        out_shape=[jax.ShapeDtypeStruct((depth, 4 * width), blocks.dtype)] * (steps + 1) + list(shapes),
-        in_specs=[anywhere] * (count + 1),
-        out_specs=[anywhere] * (count + steps + 1),
-        scratch_shapes=[dma((count, CHIPS)), dma((count, CHIPS)),
-                        dma((steps + 1, 2)), dma((steps + 1, 2)),
-                        dma((steps + 1, 2)), dma((steps + 1, 2)), dma((count + 2,))],
-        compiler_params=pltpu.CompilerParams(
-            collective_id=collective_id, has_side_effects=True
-        ),
-        cost_estimate=pl.CostEstimate(flops=0, bytes_accessed=350_000_000, transcendentals=0),
-    )(blocks, *sources)
-
-
 def to_arrival(info, x_ref, y_ref):
     width = x_ref.shape[1] // 4
     core = info[1]
@@ -388,29 +298,38 @@
         [frozen_view(depth, width)], [frozen],
         [jax.ShapeDtypeStruct((2, depth, 2 * width), bf16)], 1, "gather", squares,
     )
+    forward = [(i, (i + PLANE) % size) for i in range(size)]
+    backward = [((i + PLANE) % size, i) for i in range(size)]
+    across = [(i, i - i % CORES + (i + 1) % CORES) for i in range(size)]
+
+    def pass_on(pair):
+        return lax.ppermute(pair[0], "dp", forward), lax.ppermute(pair[1], "dp", backward)
+
+    def with_other(pair):
+        falling, rising = (lax.ppermute(part, "dp", across) for part in pair)
+        return jnp.concatenate([pair[0], falling, pair[1], rising], axis=1)
+
     rank_act = jnp.dot(tokens, down, preferred_element_type=f32).astype(bf16)
-    steps = 1
-    *weights, tokens_part, cotangent_part, rank_part = ring_exchange(
-        blocks, steps, [rows_to_columns(depth), whole_rows, whole_rows],
+    blocks, tokens, cotangent, squares = lax.optimization_barrier(
+        (blocks, tokens, cotangent, squares)
+    )
+    own = (blocks[0], blocks[1])
+    arriving = pass_on(own)
+    own_weight = with_other(own)
+    tokens_part, cotangent_part, rank_part = exchange(
+        [rows_to_columns(depth), whole_rows, whole_rows],
         [tokens, reorder(to_arrival, [cotangent], bf16, True, info, planes),
          jnp.pad(rank_act, ((0, 0), (0, 128 - rank_act.shape[1] % 128)))],
         [jax.ShapeDtypeStruct((CHIPS * rows, depth), bf16),
          jax.ShapeDtypeStruct((CHIPS * rows, outputs), bf16),
          jax.ShapeDtypeStruct((CHIPS * rows, 128), bf16)], 2,
     )
-
-    forward = [(i, (i + PLANE) % size) for i in range(size)]
-    backward = [((i + PLANE) % size, i) for i in range(size)]
-    across = [(i, i - i % CORES + (i + 1) % CORES) for i in range(size)]
-
-    def pass_on(pair):
-        return lax.ppermute(pair[0], "dp", forward), lax.ppermute(pair[1], "dp", backward)
-
-    def with_other(pair):
-        falling, rising = (lax.ppermute(part, "dp", across) for part in pair)
-        return jnp.concatenate([pair[0], falling, pair[1], rising], axis=1)
-
-    arriving = pass_on((weights[steps][:, : 2 * width], weights[steps][:, 4 * width : 6 * width]))
+    arriving, own_weight, tokens_part, cotangent_part, rank_part = lax.optimization_barrier(
+        (arriving, own_weight, tokens_part, cotangent_part, rank_part)
+    )
+    steps = 1
+    pair, arriving = arriving, pass_on(arriving)
+    weights = [own_weight, with_other(pair)]
 
     norm = jnp.sqrt(squares[:, :, 0, :].transpose(1, 0, 2).reshape(outputs) + epsilon)
     scale = magnitude.astype(f32) / norm

time: 582 us -> 516 us (0.89); the launches traced: 575 us -> 514 us
  Pallas kernels: 382 us -> 296 us
  waiting for transfers between devices: 24.5 us -> 44.2 us
  matrix products: 80.4 us -> 72.2 us
  local copies, waits for them, and re-layouts: 43 us -> 50.1 us
    pallas_call x1 -> x0, Pallas kernels: 175 us -> none  [ring_exchange(): pl.pallas_call(functools.partial(ring_kernel, views, steps), out_shape=[j...]
    pallas_call x3 -> x4, Pallas kernels: 174 us -> 263 us  [exchange(): pl.pallas_call(functools.partial(exchange_kernel, views, vector), out_sha...]
    ppermute x2 -> x3, waiting for transfers between devices: 24.4 us -> 44.2 us  [pass_on(): lax.ppermute(pair[1], 'dp', backward)]
    dot_general x12, matrix products: 72.2 us -> 63.9 us  [dot(): lax.dot_general(a, b, ((contract[:1], contract[1:]), ((), ())), preferred...]
    concatenate x0 -> x1, other arithmetic: none -> 6.93 us  [with_other(): return jnp.concatenate([pair[0], falling, pair[1], rising], axis=1)]
    unnamed x60 -> x61, local copies, waits for them, and re-layouts: 29.5 us -> 36 us
  transfers between devices with their start and end apart: 8 -> 14, of which waited for: 2 -> 2; matrix products, arithmetic and copies ran while one was open for 16% -> 19% of each run, Pallas kernels for 7% -> 27%
where the time goes in v5:
time: 516 us; the launch traced here: 514 us
  Pallas kernels  296 us (57%)
  matrix products  72.2 us (14%)
  local copies, waits for them, and re-layouts  50.1 us (10%)
  waiting for transfers between devices  44.2 us (9%)
  other arithmetic  37.4 us (7%)
  starting transfers between devices  13.2 us (3%)
    pallas_call x4, Pallas kernels, exchange(): pl.pallas_call(functools.partial(exchange_kernel, views, vector), out_sha...  263 us
    dot_general x12, matrix products, dot(): lax.dot_general(a, b, ((contract[:1], contract[1:]), ((), ())), preferred...  63.9 us
    ppermute x3, waiting for transfers between devices, pass_on(): lax.ppermute(pair[1], 'dp', backward)  44.2 us
    unnamed x61, local copies, waits for them, and re-layouts  36 us
    pallas_call x6, Pallas kernels, reorder(): pl.pallas_call(kernel, out_shape=jax.ShapeDtypeStruct((rows, outputs), ki...  33.6 us
    ppermute x3, starting transfers between devices, pass_on(): lax.ppermute(pair[1], 'dp', backward)  10.6 us
  transfers between devices with their start and end apart: 14, of which 2 were waited for; matrix products, arithmetic and copies ran while one was open for 19% of the time, Pallas kernels for 27%

profile of v5, /device:TPU:0, one launch (start us, length us, event | category | flops | bytes accessed | tf_op | source)
XLA Modules:
  0.0 514.4 jit_solution(13644341543992706572)
XLA Ops:
  0.7 6.2 %copy.14 = bf16[14336,128]{0,1:T(8,128)(2,1)} copy(bf16[14336,128]{1,0:T(8,128)(2,1)} %refs_0_.1) | data formatting | bytes 7340032 | tf_op args[1]
  10.8 48.8 %shard_map.101 = (bf16[2,3584,256]{2,1,0:T(8,128)(2,1)}, f32[8,4,8,128]{3,2,1,0:T(8,128)}) custom-call(bf16[14336,128]{1,0:T(8,128)(2,1)} %refs_0_.1, f32[8,128]{1,0:T(8,128)} %broadcast_in_dim.8.refs_1_), custom_call_target="tpu_custom_call" | custom-call | bytes 146800640 | tf_op jit(solution)/shard_map/pallas_call | solution.py:175
  68.7 5.5 %shard_map.105 = bf16[64,4096]{1,0:T(8,128)(2,1)} custom-call(s32[2]{0:T(128)} %pad_add_fusion.info, bf16[64,4096]{1,0:T(8,128)(2,1)} %x_ref.2), custom_call_target="tpu_custom_call" | custom-call | tf_op jit(solution)/shard_map/pallas_call | solution.py:224
  74.2 5.9 %shard_map.102.refs_1_ = bf16[128,4096]{1,0:T(8,128)(2,1)} custom-call(s32[2]{0:T(128)} %pad_add_fusion.info, bf16[128,4096]{1,0:T(8,128)(2,1)} %x_ref.1), custom_call_target="tpu_custom_call" | custom-call | tf_op jit(solution)/shard_map/pallas_call | solution.py:224
  81.8 4.8 shard_map.104
  90.3 89.0 %shard_map.103 = (bf16[512,3584]{1,0:T(8,128)(2,1)}, bf16[512,4096]{1,0:T(8,128)(2,1)}, bf16[512,128]{1,0:T(8,128)(2,1)}) custom-call(bf16[128,14336]{1,0:T(8,128)(2,1)} %refs_0_.2, bf16[128,4096]{1,0:T(8,128)(2,1)} %shard_map.102.refs_1_, bf16[128,128]{1,0:T(8,128)(2,1)} %pad.4.refs_2_), custom_call_target="tpu_custom_call" | custom-call | bytes 319815680 | tf_op jit(solution)/shard_map/pallas_call | solution.py:175
  179.4 6.9 %pad_maximum_fusion = bf16[3584,1024]{1,0:T(8,128)(2,1)} fusion(bf16[3584,256]{1,0:T(8,128)(2,1)} %collective-permute-done.3, bf16[3584,256]{1,0:T(8,128)(2,1)} %get-tuple-element.75, bf16[3584,256]{1,0:T(8,128)(2,1)} %collective-permute-done.2, bf16[3584,256]{1,0:T(8,128)(2,1)} %get-tuple-element.76), kind=kLoop, calls=%fused_computation.4 | loop fusion | flops 29360128 | bytes 14680064 | tf_op jit(solution)/shard_map/concatenate | solution.py:310
  199.2 9.6 %convolution_add_fusion.1 = f32[512,3584]{1,0:T(8,128)} fusion(f32[512,3584]{1,0:T(8,128)S(1)} %fusion.9, bf16[3584,1024]{1,0:T(8,128)(2,1)} %pad_maximum_fusion, bf16[512,4096]{1,0:T(8,128)(2,1)S(1)} %multiply_convert_fusion), kind=kOutput, calls=%fused_computation.7 | convolution fusion | flops 3759931392 | bytes 23068672 | tf_op jit(solution)/shard_map/dot_general | solution.py:277
  209.5 5.9 %shard_map.106 = f32[64,4096]{1,0:T(8,128)} custom-call(s32[2]{0:T(128)} %pad_add_fusion.info, f32[64,4096]{1,0:T(8,128)} %fusion.11.x_ref), custom_call_target="tpu_custom_call" | custom-call | tf_op jit(solution)/shard_map/pallas_call | solution.py:224
  217.5 7.9 %fusion.16 = f32[512,1024]{1,0:T(8,128)S(1)} fusion(bf16[512,3584]{1,0:T(8,128)(2,1)} %get-tuple-element.52, bf16[3584,1024]{1,0:T(8,128)(2,1)} %pad_maximum_fusion), kind=kOutput, calls=%fused_computation.58 | convolution fusion | flops 3758096384 | bytes 13107200 | tf_op jit(solution)/shard_map/dot_general | solution.py:277
  230.7 8.7 %convolution_add_fusion = f32[512,3584]{1,0:T(8,128)} fusion(f32[512,3584]{1,0:T(8,128)} %convolution_add_fusion.1, bf16[3584,1024]{1,0:T(8,128)(2,1)S(1)} %constant_dynamic-update-slice_fusion, bf16[512,4096]{1,0:T(8,128)(2,1)} %copy-done.2), kind=kOutput, calls=%fused_computation.6 | convolution fusion | flops 3759931392 | bytes 23068672 | tf_op jit(solution)/shard_map/dot_general | solution.py:277
  239.4 5.8 %multiply_reduce_fusion.3 = (f32[1024]{0:T(1024)S(1)}, f32[1024]{0:T(1024)S(1)}, bf16[512,1024]{1,0:T(8,128)(2,1)S(1)}, bf16[512,1024]{1,0:T(8,128)(2,1)S(1)}) fusion(bf16[512,4096]{1,0:T(8,128)(2,1)} %get-tuple-element.49, f32[512,1024]{1,0:T(8,128)S(1)} %fusion.16, bf16[512,3584]{1,0:T(8,128)(2,1)S(1)} %copy-done.10, ...), kind=kOutput, calls=%fused_computation.17 | convolution fusion | flops 3762288640 | bytes 17309696 | tf_op jit(solution)/shard_map/dot_general | solution.py:277
  246.7 24.7 %collective-permute-done.5 = bf16[3584,256]{1,0:T(8,128)(2,1)} collective-permute-done((bf16[3584,256]{1,0:T(8,128)(2,1)}, bf16[3584,256]{1,0:T(8,128)(2,1)}, u32[]{:S(2)}, u32[]{:S(2)}) %collective-permute-start.5) | collective-permute-done | bytes 1835040 | tf_op jit(solution)/shard_map/ppermute | solution.py:306
  275.7 25.6 %shard_map.107 = bf16[4,128,2048]{2,1,0:T(8,128)(2,1)} custom-call(bf16[512,2048]{1,0:T(8,128)(2,1)} %pad_maximum_fusion.1.refs_0_), custom_call_target="tpu_custom_call" | custom-call | bytes 83886080 | tf_op jit(solution)/shard_map/pallas_call | solution.py:175
  310.0 6.1 %fusion.5 = f32[512,3584]{1,0:T(8,128)} fusion(bf16[3584,1024]{1,0:T(8,128)(2,1)S(1)} %constant_dynamic-update-slice_fusion.4, bf16[512,4096]{1,0:T(8,128)(2,1)S(1)} %copy-done.3), kind=kOutput, calls=%fused_computation.27 | convolution fusion | flops 3758096384 | bytes 15728640 | tf_op jit(solution)/shard_map/dot_general | solution.py:277
  316.1 9.6 %add.62 = f32[512,3584]{1,0:T(8,128)} add(f32[512,3584]{1,0:T(8,128)} %convolution_add_fusion, f32[512,3584]{1,0:T(8,128)} %fusion.5) | non-fusion elementwise | flops 1835008 | bytes 22020096 | tf_op jit(solution)/shard_map/add | solution.py:362
  325.7 9.2 %multiply_reduce_fusion.2 = (f32[1024]{0:T(1024)S(1)}, bf16[512,1024]{1,0:T(8,128)(2,1)}) fusion(bf16[512,4096]{1,0:T(8,128)(2,1)S(1)} %copy-done.8, bf16[512,3584]{1,0:T(8,128)(2,1)} %get-tuple-element.52, bf16[3584,1024]{1,0:T(8,128)(2,1)} %copy-done.17), kind=kOutput, calls=%fused_computation.16 | convolution fusion | flops 3760192512 | bytes 13111296 | tf_op jit(solution)/shard_map/dot_general | solution.py:277
  334.9 19.5 %collective-permute-done.9 = bf16[3584,256]{1,0:T(8,128)(2,1)} collective-permute-done((bf16[3584,256]{1,0:T(8,128)(2,1)}, bf16[3584,256]{1,0:T(8,128)(2,1)}, u32[]{:S(2)}, u32[]{:S(2)}) %collective-permute-start.9) | collective-permute-done | bytes 1835040 | tf_op jit(solution)/shard_map/ppermute | solution.py:306
  361.7 4.9 multiply_reduce_fusion.1
  366.7 6.1 %fusion.3 = f32[512,3584]{1,0:T(8,128)} fusion(bf16[3584,1024]{1,0:T(8,128)(2,1)S(1)} %constant_dynamic-update-slice_fusion.8, bf16[512,4096]{1,0:T(8,128)(2,1)S(1)} %copy-done.3), kind=kOutput, calls=%fused_computation.25 | convolution fusion | flops 3758096384 | bytes 15728640 | tf_op jit(solution)/shard_map/dot_general | solution.py:277
  373.4 4.8 shard_map.108
  379.7 8.1 %add_convert_fusion.refs_1_ = bf16[512,3584]{1,0:T(8,128)(2,1)} fusion(f32[512,3584]{1,0:T(8,128)} %add.62, f32[512,3584]{1,0:T(8,128)} %fusion.3), kind=kLoop, calls=%fused_computation.5 | loop fusion | flops 3670016 | bytes 18350080 | tf_op jit(solution)/shard_map/convert_element_type | solution.py:392
  389.4 99.2 %shard_map.109 = (bf16[4,128,2048]{2,1,0:T(8,128)(2,1)}, bf16[128,14336]{1,0:T(8,128)(2,1)}, f32[32,128]{1,0:T(8,128)}, f32[2,4,4,8,4608]{4,3,2,1,0:T(8,128)}) custom-call(bf16[512,2048]{1,0:T(8,128)(2,1)} %pad_maximum_fusion.2.refs_0_, bf16[512,3584]{1,0:T(8,128)(2,1)} %add_convert_fusion.refs_1_, f32[32,128]{1,0:T(8,128)} %bitcast_multiply_fusion.refs_2_, ...), custom_call_target="tpu_custom_call" | custom-call | bytes 230686720 | tf_op jit(solution)/shard_map/pallas_call | solution.py:175
  503.5 6.7 %shard_map.110 = bf16[128,4096]{1,0:T(8,128)(2,1)} custom-call(s32[2]{0:T(128)} %pad_add_fusion.info, f32[128,4096]{1,0:T(8,128)} %pad_maximum_fusion.3.x_ref, f32[128,4096]{1,0:T(8,128)} %get-tuple-element.87.adapter_ref, f32[1,4096]{1,0:T(1,128)} %bitcast.72), custom_call_target="tpu_custom_call" | custom-call | tf_op jit(solution)/shard_map/pallas_call | solution.py:224
  (125 shorter events, 83.8 us)
Async XLA Ops:
  59.6 21.4 %copy-start.21 = (bf16[4096]{0:T(1024)(128)(2,1)S(1)}, bf16[4096]{0:T(1024)(128)(2,1)}, u32[]{:S(2)}) copy-start(bf16[4096]{0:T(1024)(128)(2,1)} %param.10) | copy-start | bytes 24580
  63.8 115.6 %collective-permute-start.2 = (bf16[3584,256]{1,0:T(8,128)(2,1)}, bf16[3584,256]{1,0:T(8,128)(2,1)}, u32[]{:S(2)}, u32[]{:S(2)}) collective-permute-start(bf16[3584,256]{1,0:T(8,128)(2,1)} %get-tuple-element.76), channel_id=1, source_target_pairs={{0,1},{1,0},{2,3},{3,2},{4,5},{5,4},{6,7},{7,6},{8,9},{9,8},{10,11... | collective-permute-start | bytes 5505032 | tf_op jit(solution)/shard_map/ppermute | solution.py:309
  63.9 115.5 %collective-permute-start.3 = (bf16[3584,256]{1,0:T(8,128)(2,1)}, bf16[3584,256]{1,0:T(8,128)(2,1)}, u32[]{:S(2)}, u32[]{:S(2)}) collective-permute-start(bf16[3584,256]{1,0:T(8,128)(2,1)} %get-tuple-element.75), channel_id=1, source_target_pairs={{0,1},{1,0},{2,3},{3,2},{4,5},{5,4},{6,7},{7,6},{8,9},{9,8},{10,11... | collective-permute-start | bytes 5505032 | tf_op jit(solution)/shard_map/ppermute | solution.py:309
  64.3 122.1 %collective-permute-start = (bf16[3584,256]{1,0:T(8,128)(2,1)}, bf16[3584,256]{1,0:T(8,128)(2,1)}, u32[]{:S(2)}, u32[]{:S(2)}) collective-permute-start(bf16[3584,256]{1,0:T(8,128)(2,1)} %get-tuple-element.76), channel_id=1, source_target_pairs={{0,8},{1,9},{2,10},{3,11},{4,12},{5,13},{6,14},{7,15},{8,16},{9,17... | collective-permute-start | bytes 5505032 | tf_op jit(solution)/shard_map/ppermute | solution.py:306
  64.8 121.5 %collective-permute-start.1 = (bf16[3584,256]{1,0:T(8,128)(2,1)}, bf16[3584,256]{1,0:T(8,128)(2,1)}, u32[]{:S(2)}, u32[]{:S(2)}) collective-permute-start(bf16[3584,256]{1,0:T(8,128)(2,1)} %get-tuple-element.75), channel_id=1, source_target_pairs={{8,0},{9,1},{10,2},{11,3},{12,4},{13,5},{14,6},{15,7},{16,8},{17,9... | collective-permute-start | bytes 5505032 | tf_op jit(solution)/shard_map/ppermute | solution.py:306
  81.1 98.3 %copy-start.18 = (f32[4096]{0:T(1024)}, f32[4096]{0:T(1024)S(1)}, u32[]{:S(2)}) copy-start(f32[4096]{0:T(1024)S(1)} %bitcast_multiply_fusion.1) | copy-start | bytes 49156
  179.4 14.0 %slice-start.3 = ((f32[8,4096]{1,0:T(8,128)}), f32[1,4096]{1,0:T(1,128)S(1)}, s32[]{:S(2)}) async-start(f32[8,4096]{1,0:T(8,128)} %shard_map.104), calls=%async_computation.3 | async-start | bytes 32768 | tf_op jit(solution)/shard_map/slice | solution.py:337
  179.4 14.0 %copy-start.7 = (bf16[512,4096]{1,0:T(8,128)(2,1)S(1)}, bf16[512,4096]{1,0:T(8,128)(2,1)}, u32[]{:S(2)}) copy-start(bf16[512,4096]{1,0:T(8,128)(2,1)} %get-tuple-element.49) | copy-start | bytes 12582916
  189.3 36.1 %collective-permute-start.6 = (bf16[3584,256]{1,0:T(8,128)(2,1)}, bf16[3584,256]{1,0:T(8,128)(2,1)}, u32[]{:S(2)}, u32[]{:S(2)}) collective-permute-start(bf16[3584,256]{1,0:T(8,128)(2,1)} %collective-permute-done), channel_id=1, source_target_pairs={{0,1},{1,0},{2,3},{3,2},{4,5},{5,4},{6,7},{7,6},{8,9},{9,8},{10,11... | collective-permute-start | bytes 5505032 | tf_op jit(solution)/shard_map/ppermute | solution.py:309
  189.3 57.4 %collective-permute-start.4 = (bf16[3584,256]{1,0:T(8,128)(2,1)}, bf16[3584,256]{1,0:T(8,128)(2,1)}, u32[]{:S(2)}, u32[]{:S(2)}) collective-permute-start(bf16[3584,256]{1,0:T(8,128)(2,1)} %collective-permute-done), channel_id=1, source_target_pairs={{0,8},{1,9},{2,10},{3,11},{4,12},{5,13},{6,14},{7,15},{8,16},{9,17... | collective-permute-start | bytes 5505032 | tf_op jit(solution)/shard_map/ppermute | solution.py:306
  189.3 39.6 %collective-permute-start.7 = (bf16[3584,256]{1,0:T(8,128)(2,1)}, bf16[3584,256]{1,0:T(8,128)(2,1)}, u32[]{:S(2)}, u32[]{:S(2)}) collective-permute-start(bf16[3584,256]{1,0:T(8,128)(2,1)} %collective-permute-done.1), channel_id=1, source_target_pairs={{0,1},{1,0},{2,3},{3,2},{4,5},{5,4},{6,7},{7,6},{8,9},{9,8},{10,11... | collective-permute-start | bytes 5505032 | tf_op jit(solution)/shard_map/ppermute | solution.py:309
  189.8 81.6 %collective-permute-start.5 = (bf16[3584,256]{1,0:T(8,128)(2,1)}, bf16[3584,256]{1,0:T(8,128)(2,1)}, u32[]{:S(2)}, u32[]{:S(2)}) collective-permute-start(bf16[3584,256]{1,0:T(8,128)(2,1)} %collective-permute-done.1), channel_id=1, source_target_pairs={{8,0},{9,1},{10,2},{11,3},{12,4},{13,5},{14,6},{15,7},{16,8},{17,9... | collective-permute-start | bytes 5505032 | tf_op jit(solution)/shard_map/ppermute | solution.py:306
  199.2 9.6 %copy-start.9 = (bf16[512,3584]{1,0:T(8,128)(2,1)S(1)}, bf16[512,3584]{1,0:T(8,128)(2,1)}, u32[]{:S(2)}) copy-start(bf16[512,3584]{1,0:T(8,128)(2,1)} %get-tuple-element.52) | copy-start | bytes 11010052
  271.4 31.7 %collective-permute-start.10 = (bf16[3584,256]{1,0:T(8,128)(2,1)}, bf16[3584,256]{1,0:T(8,128)(2,1)}, u32[]{:S(2)}, u32[]{:S(2)}) collective-permute-start(bf16[3584,256]{1,0:T(8,128)(2,1)} %collective-permute-done.4), channel_id=1, source_target_pairs={{0,1},{1,0},{2,3},{3,2},{4,5},{5,4},{6,7},{7,6},{8,9},{9,8},{10,11... | collective-permute-start | bytes 5505032 | tf_op jit(solution)/shard_map/ppermute | solution.py:309
  271.4 35.4 %collective-permute-start.11 = (bf16[3584,256]{1,0:T(8,128)(2,1)}, bf16[3584,256]{1,0:T(8,128)(2,1)S(1)}, u32[]{:S(2)}, u32[]{:S(2)}) collective-permute-start(bf16[3584,256]{1,0:T(8,128)(2,1)} %collective-permute-done.5), channel_id=1, source_target_pairs={{0,1},{1,0},{2,3},{3,2},{4,5},{5,4},{6,7},{7,6},{8,9},{9,8},{10,11... | collective-permute-start | bytes 5505032 | tf_op jit(solution)/shard_map/ppermute | solution.py:309
  271.9 63.0 %collective-permute-start.8 = (bf16[3584,256]{1,0:T(8,128)(2,1)}, bf16[3584,256]{1,0:T(8,128)(2,1)}, u32[]{:S(2)}, u32[]{:S(2)}) collective-permute-start(bf16[3584,256]{1,0:T(8,128)(2,1)} %collective-permute-done.4), channel_id=1, source_target_pairs={{0,8},{1,9},{2,10},{3,11},{4,12},{5,13},{6,14},{7,15},{8,16},{9,17... | collective-permute-start | bytes 5505032 | tf_op jit(solution)/shard_map/ppermute | solution.py:306
  271.9 82.5 %collective-permute-start.9 = (bf16[3584,256]{1,0:T(8,128)(2,1)}, bf16[3584,256]{1,0:T(8,128)(2,1)}, u32[]{:S(2)}, u32[]{:S(2)}) collective-permute-start(bf16[3584,256]{1,0:T(8,128)(2,1)} %collective-permute-done.5), channel_id=1, source_target_pairs={{8,0},{9,1},{10,2},{11,3},{12,4},{13,5},{14,6},{15,7},{16,8},{17,9... | collective-permute-start | bytes 5505032 | tf_op jit(solution)/shard_map/ppermute | solution.py:306
  316.1 9.6 %copy-start.8 = (bf16[512,4096]{1,0:T(8,128)(2,1)S(1)}, bf16[512,4096]{1,0:T(8,128)(2,1)}, u32[]{:S(2)}) copy-start(bf16[512,4096]{1,0:T(8,128)(2,1)} %get-tuple-element.49) | copy-start | bytes 12582916
  325.7 29.2 %copy-start.6 = (bf16[128,4096]{1,0:T(8,128)(2,1)S(1)}, bf16[128,4096]{1,0:T(8,128)(2,1)}, u32[]{:S(2)}) copy-start(bf16[128,4096]{1,0:T(8,128)(2,1)} %x_ref.1) | copy-start | bytes 3145732
  325.7 29.2 %copy-start.13 = (bf16[64,4096]{1,0:T(8,128)(2,1)S(1)}, bf16[64,4096]{1,0:T(8,128)(2,1)}, u32[]{:S(2)}) copy-start(bf16[64,4096]{1,0:T(8,128)(2,1)} %x_ref.2) | copy-start | bytes 1572868
  334.9 21.8 %copy-start.5 = (bf16[4,128,2048]{2,1,0:T(8,128)(2,1)S(1)}, bf16[4,128,2048]{2,1,0:T(8,128)(2,1)}, u32[]{:S(2)}) copy-start(bf16[4,128,2048]{2,1,0:T(8,128)(2,1)} %shard_map.107) | copy-start | bytes 6291460
  354.4 4.5 collective-permute-start.12
  354.4 6.7 %collective-permute-start.13 = (bf16[3584,256]{1,0:T(8,128)(2,1)}, bf16[3584,256]{1,0:T(8,128)(2,1)S(1)}, u32[]{:S(2)}, u32[]{:S(2)}) collective-permute-start(bf16[3584,256]{1,0:T(8,128)(2,1)} %collective-permute-done.9), channel_id=1, source_target_pairs={{0,1},{1,0},{2,3},{3,2},{4,5},{5,4},{6,7},{7,6},{8,9},{9,8},{10,11... | collective-permute-start | bytes 5505032 | tf_op jit(solution)/shard_map/ppermute | solution.py:309
  503.5 10.9 %copy-start.1 = (bf16[14336,64]{0,1:T(8,128)(2,1)S(1)}, bf16[14336,64]{0,1:T(8,128)(2,1)}, u32[]{:S(2)}) copy-start(bf16[14336,64]{0,1:T(8,128)(2,1)} %param.8) | copy-start | bytes 5505028
  (16 other events, 79.9 us)
